TPU v7x, 512 devices: a whole 4x8x8 slice. The times are simulated.
512 devices in a mesh: gx: 16 (over x_hi, y), gy: 16 (over z, x_lo), dev: 2 (over core).
Axes of the slice: x: 4 (x_hi: 2, x_lo: 2; x = x_hi * 2 + x_lo), y: 8, z: 8, core: 2. Of those that a mesh axis runs over, the one named last changes fastest.
Arguments:
- fine_now: float32 [3, 8, 256, 4096], P(None, 'dev', 'gx', 'gy'), may hold values from -6 to 6
- fine_before: float32 [3, 8, 256, 4096], P(None, 'dev', 'gx', 'gy'), may hold values from -6 to 6
- fine_material: float32 [4, 8, 256, 4096], P(None, 'dev', 'gx', 'gy'), may hold values from 0.5 to 2
- coarse_now: float32 [3, 16, 128, 2048], P(None, 'dev', 'gx', 'gy'), may hold values from -6 to 6
- coarse_before: float32 [3, 16, 128, 2048], P(None, 'dev', 'gx', 'gy'), may hold values from -6 to 6
- coarse_material: float32 [3, 16, 128, 2048], P(None, 'dev', 'gx', 'gy'), may hold values from 0.5 to 2
Outputs:
- fine_after: float32 [3, 8, 256, 4096], P(None, 'dev', 'gx', 'gy')
- coarse_after: float32 [3, 16, 128, 2048], P(None, 'dev', 'gx', 'gy')
All inputs are finite; a program needn't handle non-finite values.
Results may differ from a plain program's by a relative error of at most 0.0001.
Values sent between devices are 32-bit elements; how exact they have to be, the bound alone decides.
A program may use at most 64 MiB of HBM per device.

v0:
```python
import jax
import jax.numpy as jnp
from jax import lax
from jax.sharding import PartitionSpec as P

STEPS = 2


time_step = 0.15


def with_halo(cells, sides, width):
    for axis, dim in sides:
        count = lax.axis_size(axis)
        ends = count - 1
        head = lax.slice_in_dim(cells, 0, width, axis=dim)
        tail = lax.slice_in_dim(cells, cells.shape[dim] - width, cells.shape[dim], axis=dim)
        cells = jnp.concatenate(
            [
                lax.ppermute(tail, axis, [(i, (i + 1) % count) for i in range(ends)]),
                cells,
                lax.ppermute(head, axis, [((i + 1) % count, i) for i in range(ends)]),
            ],
            axis=dim,
        )
    return cells


def swapped(value, axis, stride):
    return lax.ppermute(value, axis, [(i, i ^ 1 << stride) for i in range(lax.axis_size(axis))])


def from_behind(value, axis, steps):
    count = lax.axis_size(axis)
    initial, last = (max(0, -steps), min(count, count - steps))
    return lax.ppermute(value, axis, [(source, source + steps) for source in range(initial, last)])


def restrict(plane):
    return plane.reshape(plane.shape[0], plane.shape[1] // 2, 2, plane.shape[2] // 2, 2).mean(
        axis=(2, 4)
    )


def prolong(plane):
    return jnp.repeat(jnp.repeat(plane, 2, axis=1), 2, axis=2)


def backward(field, direction):
    inner = field[1:, 1:, 1:]
    if direction == 0:
        return inner - field[:-1, 1:, 1:]
    if direction == 1:
        return inner - field[1:, :-1, 1:]
    return inner - field[1:, 1:, :-1]


def forces(padded, medium, spacing, stretched):
    centre = padded[:, :-1, :-1, :-1]
    medium_cells = medium[:, :, :-1, :-1]
    if stretched:
        vertical = medium_cells[3] / spacing
        outward = medium[3, 1:, 1:-1, 1:-1] / spacing
    else:
        vertical = 1.0 / spacing
        outward = 1.0 / spacing
    along_z = (padded[:, 1:, :-1, :-1] - centre) * vertical
    along_x = (padded[:, :-1, 1:, :-1] - centre) / spacing
    along_y = (padded[:, :-1, :-1, 1:] - centre) / spacing
    rigidity = medium_cells[1]
    lame_first = medium_cells[2]
    dilation = along_x[0] + along_y[1] + along_z[2]
    normal_x = lame_first * dilation + 2.0 * rigidity * along_x[0]
    normal_y = lame_first * dilation + 2.0 * rigidity * along_y[1]
    normal_z = lame_first * dilation + 2.0 * rigidity * along_z[2]
    shear_xy = rigidity * (along_y[0] + along_x[1])
    shear_xz = rigidity * (along_z[0] + along_x[2])
    shear_yz = rigidity * (along_z[1] + along_y[2])
    force_x = (backward(normal_x, 1) + backward(shear_xy, 2)) / spacing + backward(
        shear_xz, 0
    ) * outward
    force_y = (backward(shear_xy, 1) + backward(normal_y, 2)) / spacing + backward(
        shear_yz, 0
    ) * outward
    force_z = (backward(shear_xz, 1) + backward(shear_yz, 2)) / spacing + backward(
        normal_z, 0
    ) * outward
    return jnp.stack([force_x, force_y, force_z])


def advance(field, before, padded, medium, density, spacing, stretched):
    return (
        2.0 * field
        - before
        + time_step * time_step * forces(padded, medium, spacing, stretched) / density
    )


def layer_sides(field):
    return with_halo(field, (("gx", 2), ("gy", 3)), 1)


def depth_pads(fine_field, coarse_field, top_device):
    fine_edge = jnp.where(top_device, fine_field[:, -1], fine_field[:, 0])
    coarse_edge = jnp.where(top_device, coarse_field[:, -1], coarse_field[:, 0])
    interface = jnp.where(top_device, coarse_field[:, 0], restrict(fine_field[:, -1]))
    fine_count = fine_edge.size
    coarse_count = coarse_edge.size
    packed = jnp.concatenate(
        [fine_edge.reshape(-1), coarse_edge.reshape(-1), interface.reshape(-1)]
    )
    arrived = swapped(packed, "dev", 0)
    fine_got = arrived[:fine_count].reshape(fine_edge.shape)
    coarse_got = arrived[fine_count : fine_count + coarse_count].reshape(coarse_edge.shape)
    interface_got = arrived[fine_count + coarse_count :].reshape(coarse_edge.shape)
    fine_upper = jnp.where(top_device, jnp.zeros_like(fine_got), fine_got)
    fine_lower = jnp.where(top_device, fine_got, prolong(interface_got))
    coarse_upper = jnp.where(top_device, interface_got, coarse_got)
    coarse_lower = jnp.where(top_device, coarse_got, jnp.zeros_like(coarse_got))
    fine_padded = jnp.concatenate([fine_upper[:, None], fine_field, fine_lower[:, None]], axis=1)
    coarse_padded = jnp.concatenate(
        [coarse_upper[:, None], coarse_field, coarse_lower[:, None]], axis=1
    )
    return (fine_padded, coarse_padded)


def per_device(fine_now, fine_before, fine_material, coarse_now, coarse_before, coarse_material):
    top_device = lax.axis_index("dev") == 0
    fine_count = fine_material[:, -1].size
    packed = jnp.concatenate([fine_material[:, -1].reshape(-1), coarse_material[:, -1].reshape(-1)])
    arrived = from_behind(packed, "dev", 1)
    fine_top = arrived[:fine_count].reshape(fine_material[:, :1].shape)
    coarse_top = jnp.where(
        top_device,
        coarse_material[:, :1],
        arrived[fine_count:].reshape(coarse_material[:, :1].shape),
    )
    fine_medium = layer_sides(jnp.concatenate([fine_top, fine_material], axis=1))
    coarse_medium = layer_sides(jnp.concatenate([coarse_top, coarse_material], axis=1))
    fine_field, fine_prior = (fine_now, fine_before)
    coarse_field, coarse_prior = (coarse_now, coarse_before)
    for instant in range(STEPS):
        fine_deep, coarse_deep = depth_pads(fine_field, coarse_field, top_device)
        fine_padded = layer_sides(fine_deep)
        coarse_padded = layer_sides(coarse_deep)
        fine_next = advance(
            fine_field, fine_prior, fine_padded, fine_medium, fine_material[0], 1.0, True
        )
        coarse_next = advance(
            coarse_field, coarse_prior, coarse_padded, coarse_medium, coarse_material[0], 2.0, False
        )
        fine_prior, fine_field = (fine_field, fine_next)
        coarse_prior, coarse_field = (coarse_field, coarse_next)
    return (fine_field, coarse_field)


def solution(mesh):
    return jax.shard_map(
        per_device,
        mesh=mesh,
        in_specs=(
            P(None, "dev", "gx", "gy"),
            P(None, "dev", "gx", "gy"),
            P(None, "dev", "gx", "gy"),
            P(None, "dev", "gx", "gy"),
            P(None, "dev", "gx", "gy"),
            P(None, "dev", "gx", "gy"),
        ),
        out_specs=(P(None, "dev", "gx", "gy"), P(None, "dev", "gx", "gy")),
        check_vma=False,
    )
```

profile of v0, /device:TPU:198, one launch (start us, length us, event | category | flops | bytes accessed | tf_op | source)
XLA Modules:
  0.0 157.0 jit_solution(8707684346545731855)
XLA Ops:
  0.6 0.9 slice_bitcast_fusion.15
  1.5 3.2 %reshape_squeeze.14 = f32[3,8,2,128,2]{4,3,2,1,0:T(8,128)S(1)} reshape(f32[3,1,16,256]{3,2,0,1:T(8,128)S(1)} %slice_bitcast_fusion.15) | data formatting | bytes 98304 | tf_op jit(solution)/shard_map/reshape;squeeze | solution.py:40
  4.7 1.1 reduce_sum.18
  5.8 0.8 bitcast_select_fusion.3
  6.6 1.9 %collective-permute-start.4 = (f32[18432]{0:T(1024)S(1)}, f32[18432]{0:T(1024)S(1)}, u32[]{:S(2)}, u32[]{:S(2)}) collective-permute-start(f32[18432]{0:T(1024)S(1)} %pad_maximum_fusion.40), channel_id=1, source_target_pairs={{0,1},{1,0},{2,3},{3,2},{4,5},{5,4},{6,7},{7,6},{8,9},{9,8},{10,11... | collective-permute-start | bytes 221192 | tf_op jit(solution)/shard_map/ppermute | solution.py:30
  8.6 0.7 slice_bitcast_fusion.24
  9.3 2.4 %collective-permute-start = (f32[19456]{0:T(1024)S(1)}, f32[19456]{0:T(1024)S(1)}, u32[]{:S(2)}, u32[]{:S(2)}) collective-permute-start(f32[19456]{0:T(1024)S(1)} %pad_maximum_fusion.39), channel_id=1, source_target_pairs={{0,1},{2,3},{4,5},{6,7},{8,9},{10,11},{12,13},{14,15},{16,17},{18,... | collective-permute-start | bytes 233480 | tf_op jit(solution)/shard_map/ppermute | solution.py:36
  11.7 0.8 slice_bitcast_fusion.14
  12.6 0.8 slice_bitcast_fusion.16
  13.9 3.5 %collective-permute-start.5 = (f32[3,6,1,256]{3,2,1,0:T(1,128)S(1)}, f32[3,6,1,256]{3,2,1,0:T(1,128)S(1)}, u32[]{:S(2)}, u32[]{:S(2)}) collective-permute-start(f32[3,6,1,256]{3,2,1,0:T(1,128)S(1)} %get-tuple-element.55), channel_id=1, source_target_pairs={{0,32},{32,64},{64,96},{96,128},{128,160},{160,192},{192,224},{224... | collective-permute-start | bytes 55304 | tf_op jit(solution)/shard_map/ppermute | solution.py:20
  17.3 6.0 %collective-permute-start.6 = (f32[3,6,1,256]{3,2,1,0:T(1,128)S(1)}, f32[3,6,1,256]{3,2,1,0:T(1,128)S(1)}, u32[]{:S(2)}, u32[]{:S(2)}) collective-permute-start(f32[3,6,1,256]{3,2,1,0:T(1,128)S(1)} %get-tuple-element.56), channel_id=1, source_target_pairs={{32,0},{64,32},{96,64},{128,96},{160,128},{192,160},{224,192},{256... | collective-permute-start | bytes 55304 | tf_op jit(solution)/shard_map/ppermute | solution.py:22
  23.4 1.9 %collective-permute-start.12 = (f32[3,10,1,128]{3,2,1,0:T(1,128)S(1)}, f32[3,10,1,128]{3,2,1,0:T(1,128)S(1)}, u32[]{:S(2)}, u32[]{:S(2)}) collective-permute-start(f32[3,10,1,128]{3,2,1,0:T(1,128)S(1)} %get-tuple-element.71), channel_id=1, source_target_pairs={{0,32},{32,64},{64,96},{96,128},{128,160},{160,192},{192,224},{224... | collective-permute-start | bytes 46088 | tf_op jit(solution)/shard_map/ppermute | solution.py:20
  25.3 7.5 %collective-permute-start.13 = (f32[3,10,1,128]{3,2,1,0:T(1,128)S(1)}, f32[3,10,1,128]{3,2,1,0:T(1,128)S(1)}, u32[]{:S(2)}, u32[]{:S(2)}) collective-permute-start(f32[3,10,1,128]{3,2,1,0:T(1,128)S(1)} %get-tuple-element.72), channel_id=1, source_target_pairs={{32,0},{64,32},{96,64},{128,96},{160,128},{192,160},{224,192},{256... | collective-permute-start | bytes 46088 | tf_op jit(solution)/shard_map/ppermute | solution.py:22
  32.9 1.9 %collective-permute-start.1 = (f32[4,5,1,256]{3,2,1,0:T(1,128)S(1)}, f32[4,5,1,256]{3,2,1,0:T(1,128)S(1)}, u32[]{:S(2)}, u32[]{:S(2)}) collective-permute-start(f32[4,5,1,256]{3,2,1,0:T(1,128)S(1)} %get-tuple-element.47), channel_id=1, source_target_pairs={{0,32},{32,64},{64,96},{96,128},{128,160},{160,192},{192,224},{224... | collective-permute-start | bytes 61448 | tf_op jit(solution)/shard_map/ppermute | solution.py:20
  35.1 5.8 %collective-permute-start.14 = (f32[3,10,10,1]{3,2,1,0:T(8,128)S(1)}, f32[3,10,10,1]{3,2,1,0:T(8,128)S(1)}, u32[]{:S(2)}, u32[]{:S(2)}) collective-permute-start(f32[3,10,10,1]{3,2,1,0:T(8,128)S(1)} %get-tuple-element.60), channel_id=1, source_target_pairs={{0,2},{2,4},{4,6},{6,8},{8,10},{10,12},{12,14},{14,16},{16,18},{18... | collective-permute-start | bytes 3608 | tf_op jit(solution)/shard_map/ppermute | solution.py:20
  40.9 8.1 %collective-permute-start.10 = (f32[3,9,1,128]{3,2,1,0:T(1,128)S(1)}, f32[3,9,1,128]{3,2,1,0:T(1,128)S(1)}, u32[]{:S(2)}, u32[]{:S(2)}) collective-permute-start(f32[3,9,1,128]{3,2,1,0:T(1,128)S(1)} %get-tuple-element.74), channel_id=1, source_target_pairs={{32,0},{64,32},{96,64},{128,96},{160,128},{192,160},{224,192},{256... | collective-permute-start | bytes 41480 | tf_op jit(solution)/shard_map/ppermute | solution.py:22
  49.1 1.9 %collective-permute-start.15 = (f32[3,10,10,1]{3,2,1,0:T(8,128)S(1)}, f32[3,10,10,1]{3,2,1,0:T(8,128)S(1)}, u32[]{:S(2)}, u32[]{:S(2)}) collective-permute-start(f32[3,10,10,1]{3,2,1,0:T(8,128)S(1)} %get-tuple-element.59), channel_id=1, source_target_pairs={{2,0},{4,2},{6,4},{8,6},{10,8},{12,10},{14,12},{16,14},{18,16},{20... | collective-permute-start | bytes 3608 | tf_op jit(solution)/shard_map/ppermute | solution.py:22
  51.3 7.9 %collective-permute-done.15 = f32[3,10,10,1]{3,2,1,0:T(8,128)S(1)} collective-permute-done((f32[3,10,10,1]{3,2,1,0:T(8,128)S(1)}, f32[3,10,10,1]{3,2,1,0:T(8,128)S(1)}, u32[]{:S(2)}, u32[]{:S(2)}) %collective-permute-start.15) | collective-permute-done | bytes 1232 | tf_op jit(solution)/shard_map/ppermute | solution.py:22
  59.3 1.9 %collective-permute-start.9 = (f32[3,9,1,128]{3,2,1,0:T(1,128)S(1)}, f32[3,9,1,128]{3,2,1,0:T(1,128)S(1)}, u32[]{:S(2)}, u32[]{:S(2)}) collective-permute-start(f32[3,9,1,128]{3,2,1,0:T(1,128)S(1)} %get-tuple-element.73), channel_id=1, source_target_pairs={{0,32},{32,64},{64,96},{96,128},{128,160},{160,192},{192,224},{224... | collective-permute-start | bytes 41480 | tf_op jit(solution)/shard_map/ppermute | solution.py:20
  61.4 7.7 %collective-permute-start.2 = (f32[4,5,1,256]{3,2,1,0:T(1,128)S(1)}, f32[4,5,1,256]{3,2,1,0:T(1,128)S(1)}, u32[]{:S(2)}, u32[]{:S(2)}) collective-permute-start(f32[4,5,1,256]{3,2,1,0:T(1,128)S(1)} %get-tuple-element.48), channel_id=1, source_target_pairs={{32,0},{64,32},{96,64},{128,96},{160,128},{192,160},{224,192},{256... | collective-permute-start | bytes 61448 | tf_op jit(solution)/shard_map/ppermute | solution.py:22
  69.3 1.9 %collective-permute-start.11 = (f32[3,9,10,1]{3,2,1,0:T(8,128)S(1)}, f32[3,9,10,1]{3,2,1,0:T(8,128)S(1)}, u32[]{:S(2)}, u32[]{:S(2)}) collective-permute-start(f32[3,9,10,1]{3,2,1,0:T(8,128)S(1)} %pad_maximum_fusion.28), channel_id=1, source_target_pairs={{0,2},{2,4},{4,6},{6,8},{8,10},{10,12},{12,14},{14,16},{16,18},{18... | collective-permute-start | bytes 3248 | tf_op jit(solution)/shard_map/ppermute | solution.py:20
  71.5 3.6 %collective-permute-start.7 = (f32[3,6,18,1]{3,2,1,0:T(8,128)S(1)}, f32[3,6,18,1]{3,2,1,0:T(8,128)S(1)}, u32[]{:S(2)}, u32[]{:S(2)}) collective-permute-start(f32[3,6,18,1]{3,2,1,0:T(8,128)S(1)} %get-tuple-element.42), channel_id=1, source_target_pairs={{0,2},{2,4},{4,6},{6,8},{8,10},{10,12},{12,14},{14,16},{16,18},{18... | collective-permute-start | bytes 3896 | tf_op jit(solution)/shard_map/ppermute | solution.py:20
  75.1 2.2 %collective-permute-start.8 = (f32[3,6,18,1]{3,2,1,0:T(8,128)S(1)}, f32[3,6,18,1]{3,2,1,0:T(8,128)S(1)}, u32[]{:S(2)}, u32[]{:S(2)}) collective-permute-start(f32[3,6,18,1]{3,2,1,0:T(8,128)S(1)} %get-tuple-element.41), channel_id=1, source_target_pairs={{2,0},{4,2},{6,4},{8,6},{10,8},{12,10},{14,12},{16,14},{18,16},{20... | collective-permute-start | bytes 3896 | tf_op jit(solution)/shard_map/ppermute | solution.py:22
  77.3 2.2 %collective-permute-done.11 = f32[3,9,10,1]{3,2,1,0:T(8,128)S(1)} collective-permute-done((f32[3,9,10,1]{3,2,1,0:T(8,128)S(1)}, f32[3,9,10,1]{3,2,1,0:T(8,128)S(1)}, u32[]{:S(2)}, u32[]{:S(2)}) %collective-permute-start.11) | collective-permute-done | bytes 1112 | tf_op jit(solution)/shard_map/ppermute | solution.py:20
  81.5 3.6 %collective-permute-start.3 = (f32[4,5,18,1]{3,2,1,0:T(8,128)S(1)}, f32[4,5,18,1]{3,2,1,0:T(8,128)S(1)}, u32[]{:S(2)}, u32[]{:S(2)}) collective-permute-start(f32[4,5,18,1]{3,2,1,0:T(8,128)S(1)} %pad_maximum_fusion.23), channel_id=1, source_target_pairs={{0,2},{2,4},{4,6},{6,8},{8,10},{10,12},{12,14},{14,16},{16,18},{18... | collective-permute-start | bytes 4328 | tf_op jit(solution)/shard_map/ppermute | solution.py:20
  85.1 1.0 collective-permute-done.7
  86.5 3.1 %collective-permute-done.3 = f32[4,5,18,1]{3,2,1,0:T(8,128)S(1)} collective-permute-done((f32[4,5,18,1]{3,2,1,0:T(8,128)S(1)}, f32[4,5,18,1]{3,2,1,0:T(8,128)S(1)}, u32[]{:S(2)}, u32[]{:S(2)}) %collective-permute-start.3) | collective-permute-done | bytes 1472 | tf_op jit(solution)/shard_map/ppermute | solution.py:20
  90.0 0.9 fusion.32
  92.2 3.9 %reshape_squeeze.15 = f32[3,8,2,128,2]{4,3,2,1,0:T(8,128)S(1)} reshape(f32[3,1,16,256]{3,2,0,1:T(8,128)} %get-tuple-element.62) | data formatting | bytes 98304 | tf_op jit(solution)/shard_map/reshape;squeeze | solution.py:40
  96.6 0.9 copy.69
  97.5 0.7 fusion.108
  98.2 1.9 %collective-permute-start.16 = (f32[18432]{0:T(1024)S(1)}, f32[18432]{0:T(1024)S(1)}, u32[]{:S(2)}, u32[]{:S(2)}) collective-permute-start(f32[18432]{0:T(1024)S(1)} %pad_maximum_fusion.41), channel_id=1, source_target_pairs={{0,1},{1,0},{2,3},{3,2},{4,5},{5,4},{6,7},{7,6},{8,9},{9,8},{10,11... | collective-permute-start | bytes 221192 | tf_op jit(solution)/shard_map/ppermute | solution.py:30
  100.1 1.2 collective-permute-done.16
  101.4 1.0 pad_maximum_fusion.52
  102.4 1.9 %collective-permute-start.21 = (f32[3,10,1,128]{3,2,1,0:T(1,128)S(1)}, f32[3,10,1,128]{3,2,1,0:T(1,128)S(1)}, u32[]{:S(2)}, u32[]{:S(2)}) collective-permute-start(f32[3,10,1,128]{3,2,1,0:T(1,128)S(1)} %get-tuple-element.69), channel_id=1, source_target_pairs={{0,32},{32,64},{64,96},{96,128},{128,160},{160,192},{192,224},{224... | collective-permute-start | bytes 46088 | tf_op jit(solution)/shard_map/ppermute | solution.py:20
  104.3 7.5 %collective-permute-start.22 = (f32[3,10,1,128]{3,2,1,0:T(1,128)S(1)}, f32[3,10,1,128]{3,2,1,0:T(1,128)S(1)}, u32[]{:S(2)}, u32[]{:S(2)}) collective-permute-start(f32[3,10,1,128]{3,2,1,0:T(1,128)S(1)} %get-tuple-element.70), channel_id=1, source_target_pairs={{32,0},{64,32},{96,64},{128,96},{160,128},{192,160},{224,192},{256... | collective-permute-start | bytes 46088 | tf_op jit(solution)/shard_map/ppermute | solution.py:22
  112.3 0.9 collective-permute-done.22
  113.2 0.9 pad_maximum_fusion.27
  114.4 5.8 %collective-permute-start.23 = (f32[3,10,10,1]{3,2,1,0:T(8,128)S(1)}, f32[3,10,10,1]{3,2,1,0:T(8,128)S(1)}, u32[]{:S(2)}, u32[]{:S(2)}) collective-permute-start(f32[3,10,10,1]{3,2,1,0:T(8,128)S(1)} %get-tuple-element.58), channel_id=1, source_target_pairs={{0,2},{2,4},{4,6},{6,8},{8,10},{10,12},{12,14},{14,16},{16,18},{18... | collective-permute-start | bytes 3608 | tf_op jit(solution)/shard_map/ppermute | solution.py:20
  120.2 1.9 %collective-permute-start.17 = (f32[3,6,1,256]{3,2,0,1:T(1,128)S(1)}, f32[3,6,1,256]{3,2,0,1:T(1,128)S(1)}, u32[]{:S(2)}, u32[]{:S(2)}) collective-permute-start(f32[3,6,1,256]{3,2,0,1:T(1,128)S(1)} %get-tuple-element.51), channel_id=1, source_target_pairs={{0,32},{32,64},{64,96},{96,128},{128,160},{160,192},{192,224},{224... | collective-permute-start | bytes 55304 | tf_op jit(solution)/shard_map/ppermute | solution.py:20
  122.2 8.6 %collective-permute-start.18 = (f32[3,6,1,256]{3,2,0,1:T(1,128)S(1)}, f32[3,6,1,256]{3,2,0,1:T(1,128)S(1)}, u32[]{:S(2)}, u32[]{:S(2)}) collective-permute-start(f32[3,6,1,256]{3,2,0,1:T(1,128)S(1)} %get-tuple-element.52), channel_id=1, source_target_pairs={{32,0},{64,32},{96,64},{128,96},{160,128},{192,160},{224,192},{256... | collective-permute-start | bytes 55304 | tf_op jit(solution)/shard_map/ppermute | solution.py:22
  130.8 1.9 %collective-permute-start.24 = (f32[3,10,10,1]{3,2,1,0:T(8,128)S(1)}, f32[3,10,10,1]{3,2,1,0:T(8,128)S(1)}, u32[]{:S(2)}, u32[]{:S(2)}) collective-permute-start(f32[3,10,10,1]{3,2,1,0:T(8,128)S(1)} %get-tuple-element.57), channel_id=1, source_target_pairs={{2,0},{4,2},{6,4},{8,6},{10,8},{12,10},{14,12},{16,14},{18,16},{20... | collective-permute-start | bytes 3608 | tf_op jit(solution)/shard_map/ppermute | solution.py:22
  133.1 7.9 %collective-permute-done.24 = f32[3,10,10,1]{3,2,1,0:T(8,128)S(1)} collective-permute-done((f32[3,10,10,1]{3,2,1,0:T(8,128)S(1)}, f32[3,10,10,1]{3,2,1,0:T(8,128)S(1)}, u32[]{:S(2)}, u32[]{:S(2)}) %collective-permute-start.24) | collective-permute-done | bytes 1232 | tf_op jit(solution)/shard_map/ppermute | solution.py:22
  142.0 1.9 %collective-permute-start.19 = (f32[3,6,18,1]{3,2,1,0:T(8,128)S(1)}, f32[3,6,18,1]{3,2,1,0:T(8,128)S(1)}, u32[]{:S(2)}, u32[]{:S(2)}) collective-permute-start(f32[3,6,18,1]{3,2,1,0:T(8,128)S(1)} %copy.82), channel_id=1, source_target_pairs={{0,2},{2,4},{4,6},{6,8},{8,10},{10,12},{12,14},{14,16},{16,18},{18... | collective-permute-start | bytes 3896 | tf_op jit(solution)/shard_map/ppermute | solution.py:20
  144.7 4.1 %collective-permute-start.20 = (f32[3,6,18,1]{3,2,0,1:T(8,128)S(1)}, f32[3,6,18,1]{3,2,0,1:T(8,128)S(1)}, u32[]{:S(2)}, u32[]{:S(2)}) collective-permute-start(f32[3,6,18,1]{3,2,0,1:T(8,128)S(1)} %slice.839), channel_id=1, source_target_pairs={{2,0},{4,2},{6,4},{8,6},{10,8},{12,10},{14,12},{16,14},{18,16},{20... | collective-permute-start | bytes 3896 | tf_op jit(solution)/shard_map/ppermute | solution.py:22
  148.8 3.5 %collective-permute-done.19 = f32[3,6,18,1]{3,2,1,0:T(8,128)S(1)} collective-permute-done((f32[3,6,18,1]{3,2,1,0:T(8,128)S(1)}, f32[3,6,18,1]{3,2,1,0:T(8,128)S(1)}, u32[]{:S(2)}, u32[]{:S(2)}) %collective-permute-start.19) | collective-permute-done | bytes 1328 | tf_op jit(solution)/shard_map/ppermute | solution.py:20
  152.6 2.1 %collective-permute-done.20 = f32[3,6,18,1]{3,2,0,1:T(8,128)S(1)} collective-permute-done((f32[3,6,18,1]{3,2,0,1:T(8,128)S(1)}, f32[3,6,18,1]{3,2,0,1:T(8,128)S(1)}, u32[]{:S(2)}, u32[]{:S(2)}) %collective-permute-start.20) | collective-permute-done | bytes 1328 | tf_op jit(solution)/shard_map/ppermute | solution.py:22
  156.3 0.7 fusion.18
  (152 shorter events, 10.6 us)
Async XLA Ops:
  0.6 4.1 %copy-start = (f32[3,4,16,256]{3,2,1,0:T(8,128)S(1)}, f32[3,4,16,256]{3,2,1,0:T(8,128)}, u32[]{:S(2)}) copy-start(f32[3,4,16,256]{3,2,1,0:T(8,128)} %param.6) | copy-start | bytes 589828
  1.5 4.3 %copy-start.7 = (f32[3,8,8,128]{3,2,1,0:T(8,128)S(1)}, f32[3,8,8,128]{3,2,1,0:T(8,128)}, u32[]{:S(2)}) copy-start(f32[3,8,8,128]{3,2,1,0:T(8,128)} %param.9) | copy-start | bytes 294916
  1.5 7.0 %slice-start = ((f32[4,4,16,256]{3,2,1,0:T(8,128)}), f32[4,1,16,256]{3,2,1,0:T(8,128)S(1)}, s32[]{:S(2)}) async-start(f32[4,4,16,256]{3,2,1,0:T(8,128)} %param.8), calls=%async_computation | async-start | bytes 131072 | tf_op jit(solution)/shard_map/slice | solution.py:130
  5.8 27.1 %copy-start.3 = (f32[4,4,16,256]{3,2,1,0:T(8,128)S(1)}, f32[4,4,16,256]{3,2,1,0:T(8,128)}, u32[]{:S(2)}) copy-start(f32[4,4,16,256]{3,2,1,0:T(8,128)} %param.8) | copy-start | bytes 786436
  5.8 29.0 %copy-start.10 = (f32[3,8,8,128]{3,2,1,0:T(8,128)S(1)}, f32[3,8,8,128]{3,2,1,0:T(8,128)}, u32[]{:S(2)}) copy-start(f32[3,8,8,128]{3,2,1,0:T(8,128)} %param.11) | copy-start | bytes 294916
  6.6 6.7 %collective-permute-start.4 = (f32[18432]{0:T(1024)S(1)}, f32[18432]{0:T(1024)S(1)}, u32[]{:S(2)}, u32[]{:S(2)}) collective-permute-start(f32[18432]{0:T(1024)S(1)} %pad_maximum_fusion.40), channel_id=1, source_target_pairs={{0,1},{1,0},{2,3},{3,2},{4,5},{5,4},{6,7},{7,6},{8,9},{9,8},{10,11... | collective-permute-start | bytes 221192 | tf_op jit(solution)/shard_map/ppermute | solution.py:30
  9.3 23.5 %collective-permute-start = (f32[19456]{0:T(1024)S(1)}, f32[19456]{0:T(1024)S(1)}, u32[]{:S(2)}, u32[]{:S(2)}) collective-permute-start(f32[19456]{0:T(1024)S(1)} %pad_maximum_fusion.39), channel_id=1, source_target_pairs={{0,1},{2,3},{4,5},{6,7},{8,9},{10,11},{12,13},{14,15},{16,17},{18,... | collective-permute-start | bytes 233480 | tf_op jit(solution)/shard_map/ppermute | solution.py:36
  12.6 78.9 %copy-start.17 = (f32[4,16,256]{2,1,0:T(8,128)}, f32[4,16,256]{2,1,0:T(8,128)S(1)}, u32[]{:S(2)}) copy-start(f32[4,16,256]{2,1,0:T(8,128)S(1)} %slice_bitcast_fusion.14) | copy-start | bytes 196612
  13.3 67.3 %copy-start.19 = (f32[8,8,128]{2,1,0:T(8,128)}, f32[8,8,128]{2,1,0:T(8,128)S(1)}, u32[]{:S(2)}) copy-start(f32[8,8,128]{2,1,0:T(8,128)S(1)} %slice_bitcast_fusion.16) | copy-start | bytes 98308
  13.9 57.4 %collective-permute-start.5 = (f32[3,6,1,256]{3,2,1,0:T(1,128)S(1)}, f32[3,6,1,256]{3,2,1,0:T(1,128)S(1)}, u32[]{:S(2)}, u32[]{:S(2)}) collective-permute-start(f32[3,6,1,256]{3,2,1,0:T(1,128)S(1)} %get-tuple-element.55), channel_id=1, source_target_pairs={{0,32},{32,64},{64,96},{96,128},{128,160},{160,192},{192,224},{224... | collective-permute-start | bytes 55304 | tf_op jit(solution)/shard_map/ppermute | solution.py:20
  17.3 53.9 %collective-permute-start.6 = (f32[3,6,1,256]{3,2,1,0:T(1,128)S(1)}, f32[3,6,1,256]{3,2,1,0:T(1,128)S(1)}, u32[]{:S(2)}, u32[]{:S(2)}) collective-permute-start(f32[3,6,1,256]{3,2,1,0:T(1,128)S(1)} %get-tuple-element.56), channel_id=1, source_target_pairs={{32,0},{64,32},{96,64},{128,96},{160,128},{192,160},{224,192},{256... | collective-permute-start | bytes 55304 | tf_op jit(solution)/shard_map/ppermute | solution.py:22
  23.4 11.5 %collective-permute-start.12 = (f32[3,10,1,128]{3,2,1,0:T(1,128)S(1)}, f32[3,10,1,128]{3,2,1,0:T(1,128)S(1)}, u32[]{:S(2)}, u32[]{:S(2)}) collective-permute-start(f32[3,10,1,128]{3,2,1,0:T(1,128)S(1)} %get-tuple-element.71), channel_id=1, source_target_pairs={{0,32},{32,64},{64,96},{96,128},{128,160},{160,192},{192,224},{224... | collective-permute-start | bytes 46088 | tf_op jit(solution)/shard_map/ppermute | solution.py:20
  25.3 9.6 %collective-permute-start.13 = (f32[3,10,1,128]{3,2,1,0:T(1,128)S(1)}, f32[3,10,1,128]{3,2,1,0:T(1,128)S(1)}, u32[]{:S(2)}, u32[]{:S(2)}) collective-permute-start(f32[3,10,1,128]{3,2,1,0:T(1,128)S(1)} %get-tuple-element.72), channel_id=1, source_target_pairs={{32,0},{64,32},{96,64},{128,96},{160,128},{192,160},{224,192},{256... | collective-permute-start | bytes 46088 | tf_op jit(solution)/shard_map/ppermute | solution.py:22
  32.9 48.4 %collective-permute-start.1 = (f32[4,5,1,256]{3,2,1,0:T(1,128)S(1)}, f32[4,5,1,256]{3,2,1,0:T(1,128)S(1)}, u32[]{:S(2)}, u32[]{:S(2)}) collective-permute-start(f32[4,5,1,256]{3,2,1,0:T(1,128)S(1)} %get-tuple-element.47), channel_id=1, source_target_pairs={{0,32},{32,64},{64,96},{96,128},{128,160},{160,192},{192,224},{224... | collective-permute-start | bytes 61448 | tf_op jit(solution)/shard_map/ppermute | solution.py:20
  35.1 13.9 %collective-permute-start.14 = (f32[3,10,10,1]{3,2,1,0:T(8,128)S(1)}, f32[3,10,10,1]{3,2,1,0:T(8,128)S(1)}, u32[]{:S(2)}, u32[]{:S(2)}) collective-permute-start(f32[3,10,10,1]{3,2,1,0:T(8,128)S(1)} %get-tuple-element.60), channel_id=1, source_target_pairs={{0,2},{2,4},{4,6},{6,8},{8,10},{10,12},{12,14},{14,16},{16,18},{18... | collective-permute-start | bytes 3608 | tf_op jit(solution)/shard_map/ppermute | solution.py:20
  40.9 20.5 %collective-permute-start.10 = (f32[3,9,1,128]{3,2,1,0:T(1,128)S(1)}, f32[3,9,1,128]{3,2,1,0:T(1,128)S(1)}, u32[]{:S(2)}, u32[]{:S(2)}) collective-permute-start(f32[3,9,1,128]{3,2,1,0:T(1,128)S(1)} %get-tuple-element.74), channel_id=1, source_target_pairs={{32,0},{64,32},{96,64},{128,96},{160,128},{192,160},{224,192},{256... | collective-permute-start | bytes 41480 | tf_op jit(solution)/shard_map/ppermute | solution.py:22
  49.1 10.2 %collective-permute-start.15 = (f32[3,10,10,1]{3,2,1,0:T(8,128)S(1)}, f32[3,10,10,1]{3,2,1,0:T(8,128)S(1)}, u32[]{:S(2)}, u32[]{:S(2)}) collective-permute-start(f32[3,10,10,1]{3,2,1,0:T(8,128)S(1)} %get-tuple-element.59), channel_id=1, source_target_pairs={{2,0},{4,2},{6,4},{8,6},{10,8},{12,10},{14,12},{16,14},{18,16},{20... | collective-permute-start | bytes 3608 | tf_op jit(solution)/shard_map/ppermute | solution.py:22
  59.3 9.8 %collective-permute-start.9 = (f32[3,9,1,128]{3,2,1,0:T(1,128)S(1)}, f32[3,9,1,128]{3,2,1,0:T(1,128)S(1)}, u32[]{:S(2)}, u32[]{:S(2)}) collective-permute-start(f32[3,9,1,128]{3,2,1,0:T(1,128)S(1)} %get-tuple-element.73), channel_id=1, source_target_pairs={{0,32},{32,64},{64,96},{96,128},{128,160},{160,192},{192,224},{224... | collective-permute-start | bytes 41480 | tf_op jit(solution)/shard_map/ppermute | solution.py:20
  61.4 19.2 %copy-start.28 = (f32[3,8,8,128]{3,2,1,0:T(8,128)S(1)}, f32[3,8,8,128]{3,2,1,0:T(8,128)}, u32[]{:S(2)}) copy-start(f32[3,8,8,128]{3,2,1,0:T(8,128)} %param.10) | copy-start | bytes 294916
  61.4 19.9 %copy-start.24 = (f32[3,9,1,128]{3,2,1,0:T(1,128)}, f32[3,9,1,128]{3,2,1,0:T(1,128)S(1)}, u32[]{:S(2)}) copy-start(f32[3,9,1,128]{3,2,1,0:T(1,128)S(1)} %collective-permute-done.10) | copy-start | bytes 41476
  61.4 19.9 %collective-permute-start.2 = (f32[4,5,1,256]{3,2,1,0:T(1,128)S(1)}, f32[4,5,1,256]{3,2,1,0:T(1,128)S(1)}, u32[]{:S(2)}, u32[]{:S(2)}) collective-permute-start(f32[4,5,1,256]{3,2,1,0:T(1,128)S(1)} %get-tuple-element.48), channel_id=1, source_target_pairs={{32,0},{64,32},{96,64},{128,96},{160,128},{192,160},{224,192},{256... | collective-permute-start | bytes 61448 | tf_op jit(solution)/shard_map/ppermute | solution.py:22
  69.1 12.2 %copy-start.26 = (f32[3,9,1,128]{3,2,1,0:T(1,128)}, f32[3,9,1,128]{3,2,1,0:T(1,128)S(1)}, u32[]{:S(2)}) copy-start(f32[3,9,1,128]{3,2,1,0:T(1,128)S(1)} %collective-permute-done.9) | copy-start | bytes 41476
  69.3 10.2 %collective-permute-start.11 = (f32[3,9,10,1]{3,2,1,0:T(8,128)S(1)}, f32[3,9,10,1]{3,2,1,0:T(8,128)S(1)}, u32[]{:S(2)}, u32[]{:S(2)}) collective-permute-start(f32[3,9,10,1]{3,2,1,0:T(8,128)S(1)} %pad_maximum_fusion.28), channel_id=1, source_target_pairs={{0,2},{2,4},{4,6},{6,8},{8,10},{10,12},{12,14},{14,16},{16,18},{18... | collective-permute-start | bytes 3248 | tf_op jit(solution)/shard_map/ppermute | solution.py:20
  71.2 8.3 %copy-start.22 = (f32[3,6,1,256]{3,2,1,0:T(1,128)}, f32[3,6,1,256]{3,2,1,0:T(1,128)S(1)}, u32[]{:S(2)}) copy-start(f32[3,6,1,256]{3,2,1,0:T(1,128)S(1)} %collective-permute-done.6) | copy-start | bytes 55300
  71.5 14.7 %collective-permute-start.7 = (f32[3,6,18,1]{3,2,1,0:T(8,128)S(1)}, f32[3,6,18,1]{3,2,1,0:T(8,128)S(1)}, u32[]{:S(2)}, u32[]{:S(2)}) collective-permute-start(f32[3,6,18,1]{3,2,1,0:T(8,128)S(1)} %get-tuple-element.42), channel_id=1, source_target_pairs={{0,2},{2,4},{4,6},{6,8},{8,10},{10,12},{12,14},{14,16},{16,18},{18... | collective-permute-start | bytes 3896 | tf_op jit(solution)/shard_map/ppermute | solution.py:20
  75.1 14.7 %collective-permute-start.8 = (f32[3,6,18,1]{3,2,1,0:T(8,128)S(1)}, f32[3,6,18,1]{3,2,1,0:T(8,128)S(1)}, u32[]{:S(2)}, u32[]{:S(2)}) collective-permute-start(f32[3,6,18,1]{3,2,1,0:T(8,128)S(1)} %get-tuple-element.41), channel_id=1, source_target_pairs={{2,0},{4,2},{6,4},{8,6},{10,8},{12,10},{14,12},{16,14},{18,16},{20... | collective-permute-start | bytes 3896 | tf_op jit(solution)/shard_map/ppermute | solution.py:22
  79.5 7.0 %copy-start.14 = (f32[3,9,10,1]{3,2,1,0:T(8,128)}, f32[3,9,10,1]{3,2,1,0:T(8,128)S(1)}, u32[]{:S(2)}) copy-start(f32[3,9,10,1]{3,2,1,0:T(8,128)S(1)} %collective-permute-done.11) | copy-start | bytes 3244
  79.5 6.6 %copy-start.23 = (f32[3,6,1,256]{3,2,1,0:T(1,128)S(1)}, f32[3,6,1,256]{3,2,1,0:T(1,128)}, u32[]{:S(2)}) copy-start(f32[3,6,1,256]{3,2,1,0:T(1,128)} %copy-done.22) | copy-start | bytes 55300
  81.5 8.1 %collective-permute-start.3 = (f32[4,5,18,1]{3,2,1,0:T(8,128)S(1)}, f32[4,5,18,1]{3,2,1,0:T(8,128)S(1)}, u32[]{:S(2)}, u32[]{:S(2)}) collective-permute-start(f32[4,5,18,1]{3,2,1,0:T(8,128)S(1)} %pad_maximum_fusion.23), channel_id=1, source_target_pairs={{0,2},{2,4},{4,6},{6,8},{8,10},{10,12},{12,14},{14,16},{16,18},{18... | collective-permute-start | bytes 4328 | tf_op jit(solution)/shard_map/ppermute | solution.py:20
  96.6 36.2 %copy-start.9 = (f32[3,8,8,128]{3,2,1,0:T(8,128)S(1)}, f32[3,8,8,128]{3,2,1,0:T(8,128)}, u32[]{:S(2)}) copy-start(f32[3,8,8,128]{3,2,1,0:T(8,128)} %fusion.57) | copy-start | bytes 294916
  98.2 3.2 %collective-permute-start.16 = (f32[18432]{0:T(1024)S(1)}, f32[18432]{0:T(1024)S(1)}, u32[]{:S(2)}, u32[]{:S(2)}) collective-permute-start(f32[18432]{0:T(1024)S(1)} %pad_maximum_fusion.41), channel_id=1, source_target_pairs={{0,1},{1,0},{2,3},{3,2},{4,5},{5,4},{6,7},{7,6},{8,9},{9,8},{10,11... | collective-permute-start | bytes 221192 | tf_op jit(solution)/shard_map/ppermute | solution.py:30
  102.4 10.0 %collective-permute-start.21 = (f32[3,10,1,128]{3,2,1,0:T(1,128)S(1)}, f32[3,10,1,128]{3,2,1,0:T(1,128)S(1)}, u32[]{:S(2)}, u32[]{:S(2)}) collective-permute-start(f32[3,10,1,128]{3,2,1,0:T(1,128)S(1)} %get-tuple-element.69), channel_id=1, source_target_pairs={{0,32},{32,64},{64,96},{96,128},{128,160},{160,192},{192,224},{224... | collective-permute-start | bytes 46088 | tf_op jit(solution)/shard_map/ppermute | solution.py:20
  104.3 9.0 %collective-permute-start.22 = (f32[3,10,1,128]{3,2,1,0:T(1,128)S(1)}, f32[3,10,1,128]{3,2,1,0:T(1,128)S(1)}, u32[]{:S(2)}, u32[]{:S(2)}) collective-permute-start(f32[3,10,1,128]{3,2,1,0:T(1,128)S(1)} %get-tuple-element.70), channel_id=1, source_target_pairs={{32,0},{64,32},{96,64},{128,96},{160,128},{192,160},{224,192},{256... | collective-permute-start | bytes 46088 | tf_op jit(solution)/shard_map/ppermute | solution.py:22
  112.1 29.1 %copy-start.6 = (f32[1,9,9,129]{3,2,1,0:T(8,128)S(1)}, f32[1,9,9,129]{3,2,1,0:T(8,128)}, u32[]{:S(2)}) copy-start(f32[1,9,9,129]{3,2,1,0:T(8,128)} %copy-done.5) | copy-start | bytes 125392
  114.2 27.2 %copy-start.11 = (f32[3,8,8,128]{3,2,1,0:T(8,128)S(1)}, f32[3,8,8,128]{3,2,1,0:T(8,128)}, u32[]{:S(2)}) copy-start(f32[3,8,8,128]{3,2,1,0:T(8,128)} %param.11) | copy-start | bytes 294916
  114.2 27.2 %copy-start.15 = (f32[3,9,10,1]{3,2,1,0:T(8,128)S(1)}, f32[3,9,10,1]{3,2,1,0:T(8,128)}, u32[]{:S(2)}) copy-start(f32[3,9,10,1]{3,2,1,0:T(8,128)} %copy-done.14) | copy-start | bytes 3244
  114.2 27.2 %copy-start.25 = (f32[3,9,1,128]{3,2,1,0:T(1,128)S(1)}, f32[3,9,1,128]{3,2,1,0:T(1,128)}, u32[]{:S(2)}) copy-start(f32[3,9,1,128]{3,2,1,0:T(1,128)} %copy-done.24) | copy-start | bytes 41476
  114.2 27.2 %copy-start.27 = (f32[3,9,1,128]{3,2,1,0:T(1,128)S(1)}, f32[3,9,1,128]{3,2,1,0:T(1,128)}, u32[]{:S(2)}) copy-start(f32[3,9,1,128]{3,2,1,0:T(1,128)} %copy-done.26) | copy-start | bytes 41476
  114.4 18.4 %collective-permute-start.23 = (f32[3,10,10,1]{3,2,1,0:T(8,128)S(1)}, f32[3,10,10,1]{3,2,1,0:T(8,128)S(1)}, u32[]{:S(2)}, u32[]{:S(2)}) collective-permute-start(f32[3,10,10,1]{3,2,1,0:T(8,128)S(1)} %get-tuple-element.58), channel_id=1, source_target_pairs={{0,2},{2,4},{4,6},{6,8},{8,10},{10,12},{12,14},{14,16},{16,18},{18... | collective-permute-start | bytes 3608 | tf_op jit(solution)/shard_map/ppermute | solution.py:20
  120.2 21.6 %collective-permute-start.17 = (f32[3,6,1,256]{3,2,0,1:T(1,128)S(1)}, f32[3,6,1,256]{3,2,0,1:T(1,128)S(1)}, u32[]{:S(2)}, u32[]{:S(2)}) collective-permute-start(f32[3,6,1,256]{3,2,0,1:T(1,128)S(1)} %get-tuple-element.51), channel_id=1, source_target_pairs={{0,32},{32,64},{64,96},{96,128},{128,160},{160,192},{192,224},{224... | collective-permute-start | bytes 55304 | tf_op jit(solution)/shard_map/ppermute | solution.py:20
  122.2 19.7 %collective-permute-start.18 = (f32[3,6,1,256]{3,2,0,1:T(1,128)S(1)}, f32[3,6,1,256]{3,2,0,1:T(1,128)S(1)}, u32[]{:S(2)}, u32[]{:S(2)}) collective-permute-start(f32[3,6,1,256]{3,2,0,1:T(1,128)S(1)} %get-tuple-element.52), channel_id=1, source_target_pairs={{32,0},{64,32},{96,64},{128,96},{160,128},{192,160},{224,192},{256... | collective-permute-start | bytes 55304 | tf_op jit(solution)/shard_map/ppermute | solution.py:22
  130.8 10.2 %collective-permute-start.24 = (f32[3,10,10,1]{3,2,1,0:T(8,128)S(1)}, f32[3,10,10,1]{3,2,1,0:T(8,128)S(1)}, u32[]{:S(2)}, u32[]{:S(2)}) collective-permute-start(f32[3,10,10,1]{3,2,1,0:T(8,128)S(1)} %get-tuple-element.57), channel_id=1, source_target_pairs={{2,0},{4,2},{6,4},{8,6},{10,8},{12,10},{14,12},{16,14},{18,16},{20... | collective-permute-start | bytes 3608 | tf_op jit(solution)/shard_map/ppermute | solution.py:22
  141.2 2.8 %copy-start.8 = (f32[3,8,8,128]{3,2,1,0:T(8,128)S(1)}, f32[3,8,8,128]{3,2,1,0:T(8,128)}, u32[]{:S(2)}) copy-start(f32[3,8,8,128]{3,2,1,0:T(8,128)} %param.9) | copy-start | bytes 294916
  141.2 2.8 %copy-start.20 = (f32[8,8,128]{2,1,0:T(8,128)S(1)}, f32[8,8,128]{2,1,0:T(8,128)}, u32[]{:S(2)}) copy-start(f32[8,8,128]{2,1,0:T(8,128)} %copy-done.19) | copy-start | bytes 98308
  141.2 11.0 %copy-start.13 = (f32[5,17,257]{2,1,0:T(8,128)S(1)}, f32[5,17,257]{2,1,0:T(8,128)}, u32[]{:S(2)}) copy-start(f32[5,17,257]{2,1,0:T(8,128)} %copy-done.12) | copy-start | bytes 262144
  142.0 10.2 %collective-permute-start.19 = (f32[3,6,18,1]{3,2,1,0:T(8,128)S(1)}, f32[3,6,18,1]{3,2,1,0:T(8,128)S(1)}, u32[]{:S(2)}, u32[]{:S(2)}) collective-permute-start(f32[3,6,18,1]{3,2,1,0:T(8,128)S(1)} %copy.82), channel_id=1, source_target_pairs={{0,2},{2,4},{4,6},{6,8},{8,10},{10,12},{12,14},{14,16},{16,18},{18... | collective-permute-start | bytes 3896 | tf_op jit(solution)/shard_map/ppermute | solution.py:20
  144.7 10.6 %copy-start.16 = (f32[5,17,257]{2,1,0:T(8,128)S(1)}, f32[5,17,257]{2,1,0:T(8,128)}, u32[]{:S(2)}) copy-start(f32[5,17,257]{2,1,0:T(8,128)} %get-tuple-element.16) | copy-start | bytes 262144
  144.7 10.1 %collective-permute-start.20 = (f32[3,6,18,1]{3,2,0,1:T(8,128)S(1)}, f32[3,6,18,1]{3,2,0,1:T(8,128)S(1)}, u32[]{:S(2)}, u32[]{:S(2)}) collective-permute-start(f32[3,6,18,1]{3,2,0,1:T(8,128)S(1)} %slice.839), channel_id=1, source_target_pairs={{2,0},{4,2},{6,4},{8,6},{10,8},{12,10},{14,12},{16,14},{18,16},{20... | collective-permute-start | bytes 3896 | tf_op jit(solution)/shard_map/ppermute | solution.py:22
  (7 other events, 8.5 us)
where the time goes:
time: 158 us; the launch traced here: 157 us
  starting transfers between devices  97.6 us (62%)
  waiting for transfers between devices  30 us (19%)
  other arithmetic  14.1 us (9%)
  local copies, waits for them, and re-layouts  13.6 us (9%)
  between operations  1.71 us (1%)
    ppermute x10, starting transfers between devices, with_halo(): lax.ppermute(head, axis, [((i + 1) % count, i) for i in range(ends)])  55.6 us
    ppermute x12, starting transfers between devices, with_halo(): lax.ppermute(tail, axis, [(i, (i + 1) % count) for i in range(ends)])  35.7 us
    ppermute x10, waiting for transfers between devices, with_halo(): lax.ppermute(head, axis, [((i + 1) % count, i) for i in range(ends)])  18.9 us
    ppermute x12, waiting for transfers between devices, with_halo(): lax.ppermute(tail, axis, [(i, (i + 1) % count) for i in range(ends)])  9.78 us
    another operation x2, local copies, waits for them, and re-layouts, restrict(): plane.reshape(plane.shape[0], plane.shape[1] // 2, 2, plane.shape[2] // 2...  7.05 us
    ppermute x2, starting transfers between devices, swapped(): lax.ppermute(value, axis, [(i, i ^ 1 << stride) for i in range(lax.axis_s...  3.84 us
  transfers between devices with their start and end apart: 25, of which 9 were waited for; matrix products, arithmetic and copies ran while one was open for 5% of the time, Pallas kernels for 0%

commit v1 on v0

v1 whole, which is shorter than its diff:
```python
import jax
import jax.numpy as jnp
from jax import lax
from jax.experimental import pallas as pl
from jax.experimental.pallas import tpu as pltpu
from jax.sharding import PartitionSpec as P

STEPS = 2
STEP_SQUARED = 0.15 * 0.15
MESH = pl.DeviceIdType.MESH
F32 = jnp.float32
BF16 = jnp.bfloat16

FR, FW = 24, 384
CR, CW = 16, 256
FL, CL = 4, 8
FQ = 10
CQ = 9

X_FINE = FQ * 16
X_COARSE = 14 * 8
X_EXTRA = 3 * 16
X_ROWS = X_FINE + X_COARSE + X_EXTRA
X_LOW_ROWS = X_FINE + X_COARSE
Y_FINE = 32
Y_COARSE = 24
C_FINE = 16
Y_ROWS = Y_FINE + Y_COARSE
C_ROWS = Y_COARSE + C_FINE
SIDES = ((-1, 0), (1, 0), (0, -1), (0, 1), (-1, -1), (-1, 1), (1, -1), (1, 1))


def iota(shape, dim):
    return lax.broadcasted_iota(jnp.int32, shape, dim)


def turned(value, shift, axis):
    shift = shift % value.shape[axis]
    return pltpu.roll(value, shift, axis) if shift else value


def parts(value):
    high = value.astype(BF16)
    rest = value - high.astype(F32)
    middle = rest.astype(BF16)
    return high, middle, (rest - middle.astype(F32)).astype(BF16)


def times_right(value, matrix):
    return sum(jnp.dot(part, matrix, preferred_element_type=F32) for part in parts(value))


def times_left(matrix, value):
    return sum(jnp.dot(matrix, part, preferred_element_type=F32) for part in parts(value))


def coarse_place(fine, half):
    halo = jnp.where(fine < half, fine // 2, fine // 2 + half)
    return jnp.where(fine < 2 * half, halo, fine // 2 + half)


def gradients_to_stress(here, below, medium, stretch, which):
    def ahead(value, axis):
        return turned(value, -1, axis)

    mu, lam = medium
    dz = [b - h for b, h in zip(below, here)]
    if stretch is not None:
        dz = [d * stretch for d in dz]
    dx = [ahead(h, 0) - h for h in here]
    dy = [ahead(h, 1) - h for h in here]
    bulk = lam * (dx[0] + dy[1] + dz[2])
    twice = mu + mu
    out = {"zz": bulk + twice * dz[2], "xz": mu * (dz[0] + dx[2]), "yz": mu * (dz[1] + dy[2])}
    if which == "all":
        out["xx"] = bulk + twice * dx[0]
        out["yy"] = bulk + twice * dy[1]
        out["xy"] = mu * (dy[0] + dx[1])
    return out


def step(count, cur, qty, before_at, scale_at, stretched, zs, write, crop):
    r0, w0 = crop

    def stress(slot, which):
        medium = (qty[3, slot], qty[4, slot])
        stretch = qty[5, slot] if stretched else None
        return gradients_to_stress(
            [cur[c, slot] for c in range(3)], [cur[c, slot + 1] for c in range(3)], medium, stretch, which
        )

    def cut(value):
        return value[r0:, w0:]

    top = stress(0, "vertical")
    for k, name in enumerate(("xz", "yz", "zz")):
        zs[k] = top[name]

    def body(slot, carry):
        s = stress(slot, "all")

        def back_x(name):
            return cut(s[name]) - cut(turned(s[name], 1, 0))

        def back_y(name):
            return cut(s[name]) - cut(turned(s[name], 1, 1))

        def back_z(k, name):
            d = cut(s[name]) - cut(zs[k])
            return d * cut(qty[5, slot]) if stretched else d

        force = (
            back_x("xx") + back_y("xy") + back_z(0, "xz"),
            back_x("xy") + back_y("yy") + back_z(1, "yz"),
            back_x("xz") + back_y("yz") + back_z(2, "zz"),
        )
        scale = cut(qty[scale_at, slot])
        for c in range(3):
            now = cut(cur[c, slot])
            write(c, slot, now + now - before_at(c, slot)[r0:, w0:] + scale * force[c])
        for k, name in enumerate(("xz", "yz", "zz")):
            zs[k] = s[name]
        return carry

    lax.fori_loop(1, count + 1, body, 0)


def pack_x(qf, qc, low, high):
    row8 = iota((8, 256), 0)
    crow = iota((8, 128), 0)

    def store(ref, at, value):
        ref[pl.ds(at, 8), :] = value[:, :128]
        ref[pl.ds(at + 8, 8), :] = value[:, 128:]

    for g in range(FQ):
        up = jnp.zeros((8, 256), F32)
        down = up
        for l in range(FL):
            z = jnp.where(row8 < 4, qf[g, l + 1, 8:16, 128:], qf[g, l + 1, 16:24, 128:])
            t = turned(z, 2 * l, 0)
            up = t if l == 0 else jnp.where(row8 // 2 == l, t, up)
            down = t if l == 0 else jnp.where(row8 // 2 == l - 1, t, down)
        store(high, g * 16, up)
        store(low, g * 16, down)
    for q in range(5):
        for half in range(2):
            for l in range(4):
                t = turned(qc[q, half * 4 + l + 1, 8:16, 128:], 2 * l, 0)
                up = t if l == 0 else jnp.where(crow // 2 == l, t, up)
                down = t if l == 0 else jnp.where(crow // 2 == l - 1, t, down)
            at = X_FINE + (q * 2 + half) * 8
            high[pl.ds(at, 8), :] = up
            low[pl.ds(at, 8), :] = down
    for q in range(4):
        for l in range(8):
            t = turned(qc[5 + q, l + 1, 8:16, 128:], l, 0)
            up = t if l == 0 else jnp.where(crow == l, t, up)
            down = t if l == 0 else jnp.where(crow == l - 1, t, down)
        at = X_FINE + (10 + q) * 8
        high[pl.ds(at, 8), :] = up
        low[pl.ds(at, 8), :] = down
    for c in range(3):
        more = jnp.where(row8 < 2, turned(qf[c, 3, 8:16, 128:], -2, 0), qf[c, 4, 8:16, 128:])
        store(high, X_FINE + X_COARSE + c * 16, more)


def unpack_x(qf, qc, low, high):
    row8 = iota((8, 256), 0)
    crow = iota((8, 128), 0)

    def load(ref, at):
        return jnp.concatenate([ref[pl.ds(at, 8), :], ref[pl.ds(at + 8, 8), :]], axis=1)

    for g in range(FQ):
        up = load(high, g * 16)
        down = load(low, g * 16)
        more = load(high, X_FINE + X_COARSE + g * 16) if g < 3 else None
        for l in range(FL):
            t = jnp.where(row8 < 4, turned(up, -2 * l, 0), turned(down, -2 * l, 0))
            if g < 3 and l == 2:
                t = jnp.where(row8 // 2 == 1, turned(more, 2, 0), t)
            if g < 3 and l == 3:
                t = jnp.where(row8 // 2 == 1, more, t)
            qf[g, l + 1, 0:8, 128:] = t
    for q in range(5):
        for half in range(2):
            at = X_FINE + (q * 2 + half) * 8
            up = high[pl.ds(at, 8), :]
            down = low[pl.ds(at, 8), :]
            for l in range(4):
                t = jnp.where(crow < 4, turned(up, -2 * l, 0), turned(down, -2 * l, 0))
                qc[q, half * 4 + l + 1, 0:8, 128:] = t
    for q in range(4):
        at = X_FINE + (10 + q) * 8
        up = high[pl.ds(at, 8), :]
        down = low[pl.ds(at, 8), :]
        for l in range(8):
            qc[5 + q, l + 1, 0:8, 128:] = jnp.where(crow < 4, turned(up, -l, 0), turned(down, -l, 0))


def pack_y(qf, qc, out):
    lane = iota((16, 128), 1)
    lane8 = iota((8, 128), 1)
    row8 = iota((8, 128), 0)
    for t in range(2):
        packed = jnp.zeros((16, 128), F32)
        for k in range(20):
            g, l = t * 5 + k // 4, k % 4
            z = jnp.where(lane < 64, qf[g, l + 1, 8:24, 128:256], qf[g, l + 1, 8:24, 256:384])
            mine = ((lane + (2 - 6 * k + 128)) & 127) < 6
            packed = jnp.where(mine, turned(z, 6 * k, 1), packed)
        out[pl.ds(t * 16, 16), :] = packed
        out[pl.ds(Y_ROWS + t * 8, 8), :] = jnp.where(row8 < 4, packed[:8], packed[8:])
    for t in range(3):
        packed = jnp.zeros((8, 128), F32)
        for k in range(32 if t < 2 else 8):
            q, l = t * 4 + k // 8, k % 8
            mine = ((lane8 + (2 - 4 * k + 128)) & 127) < 4
            packed = jnp.where(mine, turned(qc[q, l + 1, 8:16, 128:256], 4 * k, 1), packed)
        out[pl.ds(Y_FINE + t * 8, 8), :] = packed


def unpack_y(qf, qc, side, corner):
    lane = iota((16, 128), 1)
    lane8 = iota((8, 128), 1)
    row8 = iota((8, 128), 0)
    fine_low = ((lane + 2) & 127) % 6 < 2
    fine_low8 = ((lane8 + 2) & 127) % 6 < 2
    coarse_low8 = ((lane8 + 2) & 127) % 4 < 2

    def corners(at, low):
        before = jnp.where(low, corner[0, pl.ds(at, 8), :], corner[1, pl.ds(at, 8), :])
        after = jnp.where(low, corner[2, pl.ds(at, 8), :], corner[3, pl.ds(at, 8), :])
        return jnp.where(row8 < 4, after, before)

    for t in range(2):
        own = jnp.where(fine_low, side[0, pl.ds(t * 16, 16), :], side[1, pl.ds(t * 16, 16), :])
        both = jnp.concatenate([corners(Y_COARSE + t * 8, fine_low8), own], axis=0)
        for k in range(20):
            g, l = t * 5 + k // 4, k % 4
            qf[g, l + 1, :, 0:128] = turned(both, -6 * k, 1)
    for t in range(3):
        at = Y_FINE + t * 8
        own = jnp.where(coarse_low8, side[0, pl.ds(at, 8), :], side[1, pl.ds(at, 8), :])
        both = jnp.concatenate([corners(t * 8, coarse_low8), own], axis=0)
        for k in range(32 if t < 2 else 8):
            q, l = t * 4 + k // 8, k % 8
            qc[q, l + 1, :, 0:128] = turned(both, -4 * k, 1)


def kernel(
    fine_now, fine_before, fine_material, coarse_now, coarse_before, coarse_material,
    fine_out, coarse_out,
    qf, qc, u1f, u1c, zf, zc,
    sx_low, sx_high, sy, rx_low, rx_high, ry, rc,
    give, got, lanes_down, lanes_up, rows_down, rows_up,
    load_sem, send_sem, recv_sem, deep_send, deep_recv,
):
    gx, gy, dev = lax.axis_index("gx"), lax.axis_index("gy"), lax.axis_index("dev")
    nx, ny = lax.axis_size("gx"), lax.axis_size("gy")
    top = dev == 0
    partner = {"gx": gx, "gy": gy, "dev": 1 - dev}
    there = []
    for dx, dy in SIDES:
        x, y = gx + dx, gy + dy
        there.append(({"gx": x, "gy": y, "dev": dev}, (x >= 0) & (x < nx) & (y >= 0) & (y < ny)))

    barrier = pltpu.get_barrier_semaphore()
    expected = 1
    pl.semaphore_signal(barrier, inc=1, device_id=partner, device_id_type=MESH)
    for where, present in there:
        @pl.when(present)
        def _(where=where):
            pl.semaphore_signal(barrier, inc=1, device_id=where, device_id_type=MESH)
        expected = expected + jnp.where(present, 1, 0)

    fine_own = (pl.ds(1, FL), pl.ds(8, 16), pl.ds(128, 256))
    coarse_own = (pl.ds(1, CL), pl.ds(8, 8), pl.ds(128, 128))
    loads = [
        (fine_now, qf.at[(pl.ds(0, 3), *fine_own)]),
        (fine_material.at[pl.ds(1, 3)], qf.at[(pl.ds(3, 3), *fine_own)]),
        (fine_before, qf.at[(pl.ds(6, 3), *fine_own)]),
        (fine_material.at[pl.ds(0, 1)], qf.at[(pl.ds(9, 1), *fine_own)]),
        (coarse_now, qc.at[(pl.ds(0, 3), *coarse_own)]),
        (coarse_material.at[pl.ds(1, 2)], qc.at[(pl.ds(3, 2), *coarse_own)]),
        (coarse_before, qc.at[(pl.ds(5, 3), *coarse_own)]),
        (coarse_material.at[pl.ds(0, 1)], qc.at[(pl.ds(8, 1), *coarse_own)]),
    ]
    copies = [pltpu.make_async_copy(src, dst, load_sem.at[k]) for k, (src, dst) in enumerate(loads)]
    for copy in copies:
        copy.start()

    def zero_unless(present, ref, at=None):
        @pl.when(jnp.logical_not(present))
        def _():
            if at is None:
                ref[...] = jnp.zeros(ref.shape, F32)
            else:
                ref[at] = jnp.zeros(ref.shape[1:], F32)

    zero_unless(there[0][1], rx_low)
    zero_unless(there[1][1], rx_high)
    for k in range(2):
        zero_unless(there[2 + k][1], ry, k)
    for k in range(4):
        zero_unless(there[4 + k][1], rc, k)

    @pl.when(top)
    def _():
        for c in range(3):
            qf[c, 0] = jnp.zeros((FR, FW), F32)
            u1f[c, 0] = jnp.zeros((FR, FW), F32)
        for k in range(3, 6):
            qf[k, 0] = jnp.zeros((FR, FW), F32)

    @pl.when(jnp.logical_not(top))
    def _():
        for c in range(3):
            qc[c, CL + 1] = jnp.zeros((CR, CW), F32)
            u1c[c, CL + 1] = jnp.zeros((CR, CW), F32)
        place = coarse_place(iota((FW, CW), 0), 64)
        lanes_down[...] = jnp.where(place == iota((FW, CW), 1), 0.5, 0.0).astype(BF16)
        place = coarse_place(iota((CW, FW), 1), 64)
        lanes_up[...] = jnp.where(place == iota((CW, FW), 0), 1.0, 0.0).astype(BF16)

        def rows(shape, fine_dim):
            fine, coarse = iota(shape, fine_dim), iota(shape, 1 - fine_dim)
            place = coarse_place(fine % FR, 4)
            return (place == coarse % CR) & (fine // FR == coarse // CR)

        rows_down[...] = jnp.where(rows((3 * CR, 3 * FR), 1), 0.5, 0.0).astype(BF16)
        rows_up[...] = jnp.where(rows((3 * FR, 3 * CR), 0), 1.0, 0.0).astype(BF16)

    for copy in copies:
        copy.wait()
    for l in range(FL):
        own = (9, l + 1, pl.ds(8, 16), pl.ds(128, 256))
        qf[own] = STEP_SQUARED / qf[own]
    for l in range(CL):
        own = (8, l + 1, pl.ds(8, 8), pl.ds(128, 128))
        qc[own] = (0.25 * STEP_SQUARED) / qc[own]
    pack_x(qf, qc, sx_low, sx_high)
    pack_y(qf, qc, sy)
    pl.semaphore_wait(barrier, expected)

    side_msg, corner_msg = sy.at[pl.ds(0, Y_ROWS)], sy.at[pl.ds(Y_FINE, C_ROWS)]
    messages = [
        (sx_high, rx_high), (sx_low, rx_low), (side_msg, ry.at[1]), (side_msg, ry.at[0]),
        (corner_msg, rc.at[3]), (corner_msg, rc.at[2]), (corner_msg, rc.at[1]), (corner_msg, rc.at[0]),
    ]
    sends = []
    for k, (src, dst) in enumerate(messages):
        copy = pltpu.make_async_remote_copy(
            src, dst, send_sem.at[k], recv_sem.at[k], device_id=there[k][0], device_id_type=MESH
        )

        @pl.when(there[k][1])
        def _(copy=copy):
            copy.start()

        sends.append(copy)

    def arrived(k):
        opposite = SIDES.index((-SIDES[k][0], -SIDES[k][1]))

        @pl.when(there[opposite][1])
        def _():
            sends[k].wait_recv()

    for k in range(8):
        arrived(k)
    unpack_x(qf, qc, rx_low, rx_high)
    unpack_y(qf, qc, ry, rc)

    def deep_exchange(phase, cur_f, cur_c):
        mine_f, theirs_f = jnp.where(top, FL, 1), jnp.where(top, 0, FL + 1)
        mine_c, theirs_c = jnp.where(top, CL, 1), jnp.where(top, 0, CL + 1)

        @pl.when(top)
        def _():
            for c in range(3):
                give[phase, c] = cur_c[c, 1]

        @pl.when(jnp.logical_not(top))
        def _():
            fine = jnp.concatenate([cur_f[c, FL] for c in range(3)], axis=0)
            small = times_left(rows_down[...], times_right(fine, lanes_down[...]))
            for c in range(3):
                give[phase, c] = small[c * CR : (c + 1) * CR]

        moves = [
            (cur_f.at[pl.ds(0, 3), mine_f], cur_f.at[pl.ds(0, 3), theirs_f]),
            (cur_c.at[pl.ds(0, 3), mine_c], cur_c.at[pl.ds(0, 3), theirs_c]),
            (give.at[phase], got.at[phase]),
        ]
        copies = [
            pltpu.make_async_remote_copy(
                src, dst, deep_send.at[phase, k], deep_recv.at[phase, k], device_id=partner, device_id_type=MESH
            )
            for k, (src, dst) in enumerate(moves)
        ]
        for copy in copies:
            copy.start()
        if phase == 0:
            medium = [
                pltpu.make_async_remote_copy(
                    src, dst, deep_send.at[0, 3 + k], deep_recv.at[0, 3 + k], device_id=partner, device_id_type=MESH
                )
                for k, (src, dst) in enumerate(
                    (
                        (qf.at[pl.ds(3, 3), FL], qf.at[pl.ds(3, 3), 0]),
                        (qc.at[pl.ds(3, 2), CL], qc.at[pl.ds(3, 2), 0]),
                    )
                )
            ]

            @pl.when(top)
            def _():
                for copy in medium:
                    copy.start()
                for k in range(3, 5):
                    qc[k, 0] = qc[k, 1]
        for copy in copies:
            copy.wait_recv()

        @pl.when(top)
        def _():
            for c in range(3):
                cur_c[c, 0] = got[phase, c]

        @pl.when(jnp.logical_not(top))
        def _():
            coarse = jnp.concatenate([got[phase, c] for c in range(3)], axis=0)
            large = times_left(rows_up[...], times_right(coarse, lanes_up[...]))
            for c in range(3):
                cur_f[c, FL + 1] = large[c * FR : (c + 1) * FR]

        for copy in copies:
            copy.wait_send()
        if phase == 0:
            @pl.when(top)
            def _():
                for copy in medium:
                    copy.wait_send()

            @pl.when(jnp.logical_not(top))
            def _():
                for copy in medium:
                    copy.wait_recv()

    deep_exchange(0, qf, qc)

    def keep_f(c, slot, value):
        u1f[c, slot] = value

    def keep_c(c, slot, value):
        u1c[c, slot] = value

    step(FL, qf, qf, lambda c, s: qf[6 + c, s], 9, True, zf, keep_f, (0, 0))
    step(CL, qc, qc, lambda c, s: qc[5 + c, s], 8, False, zc, keep_c, (0, 0))

    deep_exchange(1, u1f, u1c)

    def out_f(c, slot, value):
        fine_out[c, slot - 1] = value

    def out_c(c, slot, value):
        coarse_out[c, slot - 1] = value

    step(FL, u1f, qf, lambda c, s: qf[c, s], 9, True, zf, out_f, (8, 128))
    step(CL, u1c, qc, lambda c, s: qc[c, s], 8, False, zc, out_c, (8, 128))

    for k, copy in enumerate(sends):
        @pl.when(there[k][1])
        def _(copy=copy):
            copy.wait_send()


def per_device(*arrays):
    fine, coarse = arrays[0], arrays[3]
    return pl.pallas_call(
        kernel,
        out_shape=(jax.ShapeDtypeStruct(fine.shape, F32), jax.ShapeDtypeStruct(coarse.shape, F32)),
        in_specs=[pl.BlockSpec(memory_space=pltpu.HBM)] * 6,
        out_specs=(pl.BlockSpec(memory_space=pltpu.VMEM), pl.BlockSpec(memory_space=pltpu.VMEM)),
        scratch_shapes=[
            pltpu.VMEM((FQ, FL + 2, FR, FW), F32),
            pltpu.VMEM((CQ, CL + 2, CR, CW), F32),
            pltpu.VMEM((3, FL + 2, FR, FW), F32),
            pltpu.VMEM((3, CL + 2, CR, CW), F32),
            pltpu.VMEM((3, FR, FW), F32),
            pltpu.VMEM((3, CR, CW), F32),
            pltpu.VMEM((X_LOW_ROWS, 128), F32),
            pltpu.VMEM((X_ROWS, 128), F32),
            pltpu.VMEM((Y_ROWS + C_FINE, 128), F32),
            pltpu.VMEM((X_LOW_ROWS, 128), F32),
            pltpu.VMEM((X_ROWS, 128), F32),
            pltpu.VMEM((2, Y_ROWS, 128), F32),
            pltpu.VMEM((4, C_ROWS, 128), F32),
            pltpu.VMEM((STEPS, 3, CR, CW), F32),
            pltpu.VMEM((STEPS, 3, CR, CW), F32),
            pltpu.VMEM((FW, CW), BF16),
            pltpu.VMEM((CW, FW), BF16),
            pltpu.VMEM((3 * CR, 3 * FR), BF16),
            pltpu.VMEM((3 * FR, 3 * CR), BF16),
            pltpu.SemaphoreType.DMA((8,)),
            pltpu.SemaphoreType.DMA((8,)),
            pltpu.SemaphoreType.DMA((8,)),
            pltpu.SemaphoreType.DMA((STEPS, 5)),
            pltpu.SemaphoreType.DMA((STEPS, 5)),
        ],
        compiler_params=pltpu.CompilerParams(
            collective_id=0, has_side_effects=True, vmem_limit_bytes=40 * 2**20
        ),
    )(*arrays)


def solution(mesh):
    spec = P(None, "dev", "gx", "gy")
    return jax.shard_map(
        per_device, mesh=mesh, in_specs=(spec,) * 6, out_specs=(spec, spec), check_vma=False
    )
```

time: 158 us -> 30.3 us (0.19)
  the two profiles are of different devices: /device:TPU:198 before, /device:TPU:249 now
where the time goes in v1:
time: 30.3 us; the launch traced here: 30 us
  Pallas kernels  22.6 us (75%)
  local copies, waits for them, and re-layouts  6.79 us (22%)
  between operations  0.65 us (2%)
    pallas_call x1, Pallas kernels, per_device(): pl.pallas_call(kernel, out_shape=(jax.ShapeDtypeStruct(fine.shape, F32),...  22.6 us
    unnamed x14, local copies, waits for them, and re-layouts  6.79 us

profile of v1, /device:TPU:249, one launch (start us, length us, event | category | flops | bytes accessed | tf_op | source)
XLA Modules:
  0.0 30.0 jit_solution(7158058007546835520)
XLA Ops:
  0.6 0.0 copy-start
  0.6 0.9 %copy-done = f32[4,4,16,256]{3,2,1,0:T(8,128)S(1)} copy-done((f32[4,4,16,256]{3,2,1,0:T(8,128)S(1)}, f32[4,4,16,256]{3,2,1,0:T(8,128)}, u32[]{:S(2)}) %copy-start) | copy-done | bytes 262168
  1.6 0.0 copy-start.1
  1.6 0.9 %copy-done.1 = f32[3,4,16,256]{3,2,1,0:T(8,128)S(1)} copy-done((f32[3,4,16,256]{3,2,1,0:T(8,128)S(1)}, f32[3,4,16,256]{3,2,1,0:T(8,128)}, u32[]{:S(2)}) %copy-start.1) | copy-done | bytes 196632
  2.5 0.0 copy-start.2
  2.5 0.9 %copy-done.2 = f32[3,4,16,256]{3,2,1,0:T(8,128)S(1)} copy-done((f32[3,4,16,256]{3,2,1,0:T(8,128)S(1)}, f32[3,4,16,256]{3,2,1,0:T(8,128)}, u32[]{:S(2)}) %copy-start.2) | copy-done | bytes 196632
  3.4 0.0 copy-start.3
  3.4 0.9 %copy-done.3 = f32[3,8,8,128]{3,2,1,0:T(8,128)S(1)} copy-done((f32[3,8,8,128]{3,2,1,0:T(8,128)S(1)}, f32[3,8,8,128]{3,2,1,0:T(8,128)}, u32[]{:S(2)}) %copy-start.3) | copy-done | bytes 98328
  4.3 0.0 copy-start.4
  4.3 0.9 %copy-done.4 = f32[3,8,8,128]{3,2,1,0:T(8,128)S(1)} copy-done((f32[3,8,8,128]{3,2,1,0:T(8,128)S(1)}, f32[3,8,8,128]{3,2,1,0:T(8,128)}, u32[]{:S(2)}) %copy-start.4) | copy-done | bytes 98328
  5.2 0.0 copy-start.5
  5.2 0.9 %copy-done.5 = f32[3,8,8,128]{3,2,1,0:T(8,128)S(1)} copy-done((f32[3,8,8,128]{3,2,1,0:T(8,128)S(1)}, f32[3,8,8,128]{3,2,1,0:T(8,128)}, u32[]{:S(2)}) %copy-start.5) | copy-done | bytes 98328
  6.1 22.6 %shard_map.77 = (f32[3,4,16,256]{3,2,1,0:T(8,128)S(1)}, f32[3,8,8,128]{3,2,1,0:T(8,128)S(1)}) custom-call(f32[3,4,16,256]{3,2,1,0:T(8,128)S(1)} %copy-done.1, f32[3,4,16,256]{3,2,1,0:T(8,128)S(1)} %copy-done.2, f32[4,4,16,256]{3,2,1,0:T(8,128)S(1)} %copy-done, f32[3,8,8,128]{3,2,1,0:T(8,128)S(1)} %copy-done.3, f32[3,8,8,128]{3,2,1,0:T(8,128)S(1)} %copy-done.4, ...), custom_call_target="tpu_custom_call" | custom-call | tf_op jit(solution)/shard_map/pallas_call | solution.py:482
  28.7 0.7 %copy.10 = f32[3,4,16,256]{3,2,1,0:T(8,128)} copy(f32[3,4,16,256]{3,2,1,0:T(8,128)S(1)} %get-tuple-element.4) | data formatting | bytes 393216
  29.4 0.6 %copy.11 = f32[3,8,8,128]{3,2,1,0:T(8,128)} copy(f32[3,8,8,128]{3,2,1,0:T(8,128)S(1)} %get-tuple-element.5) | data formatting | bytes 196608
Async XLA Ops:
  0.6 1.0 %copy-start = (f32[4,4,16,256]{3,2,1,0:T(8,128)S(1)}, f32[4,4,16,256]{3,2,1,0:T(8,128)}, u32[]{:S(2)}) copy-start(f32[4,4,16,256]{3,2,1,0:T(8,128)} %fine_material.1) | copy-start | bytes 786436
  1.6 0.9 %copy-start.1 = (f32[3,4,16,256]{3,2,1,0:T(8,128)S(1)}, f32[3,4,16,256]{3,2,1,0:T(8,128)}, u32[]{:S(2)}) copy-start(f32[3,4,16,256]{3,2,1,0:T(8,128)} %fine_now.1) | copy-start | bytes 589828
  2.5 0.9 %copy-start.2 = (f32[3,4,16,256]{3,2,1,0:T(8,128)S(1)}, f32[3,4,16,256]{3,2,1,0:T(8,128)}, u32[]{:S(2)}) copy-start(f32[3,4,16,256]{3,2,1,0:T(8,128)} %fine_before.1) | copy-start | bytes 589828
  3.4 0.9 %copy-start.3 = (f32[3,8,8,128]{3,2,1,0:T(8,128)S(1)}, f32[3,8,8,128]{3,2,1,0:T(8,128)}, u32[]{:S(2)}) copy-start(f32[3,8,8,128]{3,2,1,0:T(8,128)} %coarse_now.1) | copy-start | bytes 294916
  4.3 0.9 %copy-start.4 = (f32[3,8,8,128]{3,2,1,0:T(8,128)S(1)}, f32[3,8,8,128]{3,2,1,0:T(8,128)}, u32[]{:S(2)}) copy-start(f32[3,8,8,128]{3,2,1,0:T(8,128)} %coarse_before.1) | copy-start | bytes 294916
  5.2 0.9 %copy-start.5 = (f32[3,8,8,128]{3,2,1,0:T(8,128)S(1)}, f32[3,8,8,128]{3,2,1,0:T(8,128)}, u32[]{:S(2)}) copy-start(f32[3,8,8,128]{3,2,1,0:T(8,128)} %coarse_material.1) | copy-start | bytes 294916

commit v2 on v1

--- a/solution.py
+++ b/solution.py
@@ -79,25 +79,27 @@
     return out
 
 
-def step(count, cur, qty, before_at, scale_at, stretched, zs, write, crop):
-    r0, w0 = crop
-
-    def stress(slot, which):
-        medium = (qty[3, slot], qty[4, slot])
-        stretch = qty[5, slot] if stretched else None
+class Step:
+    def __init__(self, count, cur, qty, before_at, scale_at, stretched, write, crop):
+        self.count, self.cur, self.qty, self.before_at = count, cur, qty, before_at
+        self.scale_at, self.stretched, self.write, self.crop = scale_at, stretched, write, crop
+
+    def cut(self, value):
+        return value[self.crop[0] :, self.crop[1] :]
+
+    def stress(self, slot, which="all"):
+        cur, qty = self.cur, self.qty
+        stretch = qty[5, slot] if self.stretched else None
         return gradients_to_stress(
-            [cur[c, slot] for c in range(3)], [cur[c, slot + 1] for c in range(3)], medium, stretch, which
+            [cur[c, slot] for c in range(3)],
+            [cur[c, slot + 1] for c in range(3)],
+            (qty[3, slot], qty[4, slot]),
+            stretch,
+            which,
         )
 
-    def cut(value):
-        return value[r0:, w0:]
-
-    top = stress(0, "vertical")
-    for k, name in enumerate(("xz", "yz", "zz")):
-        zs[k] = top[name]
-
-    def body(slot, carry):
-        s = stress(slot, "all")
+    def move(self, slot, s, above):
+        cut = self.cut
 
         def back_x(name):
             return cut(s[name]) - cut(turned(s[name], 1, 0))
@@ -105,24 +107,33 @@
         def back_y(name):
             return cut(s[name]) - cut(turned(s[name], 1, 1))
 
-        def back_z(k, name):
-            d = cut(s[name]) - cut(zs[k])
-            return d * cut(qty[5, slot]) if stretched else d
+        def back_z(name):
+            d = cut(s[name]) - cut(above[name])
+            return d * cut(self.qty[5, slot]) if self.stretched else d
 
         force = (
-            back_x("xx") + back_y("xy") + back_z(0, "xz"),
-            back_x("xy") + back_y("yy") + back_z(1, "yz"),
-            back_x("xz") + back_y("yz") + back_z(2, "zz"),
+            back_x("xx") + back_y("xy") + back_z("xz"),
+            back_x("xy") + back_y("yy") + back_z("yz"),
+            back_x("xz") + back_y("yz") + back_z("zz"),
         )
-        scale = cut(qty[scale_at, slot])
+        scale = cut(self.qty[self.scale_at, slot])
         for c in range(3):
-            now = cut(cur[c, slot])
-            write(c, slot, now + now - before_at(c, slot)[r0:, w0:] + scale * force[c])
-        for k, name in enumerate(("xz", "yz", "zz")):
-            zs[k] = s[name]
-        return carry
-
-    lax.fori_loop(1, count + 1, body, 0)
+            now = cut(self.cur[c, slot])
+            before = cut(self.before_at(c, slot))
+            self.write(c, slot, now + now - before + scale * force[c])
+
+    def inner(self):
+        self.first = above = self.stress(1)
+        for slot in range(2, self.count):
+            s = self.stress(slot)
+            self.move(slot, s, above)
+            above = s
+        self.above = above
+
+    def outer(self):
+        last = self.stress(self.count)
+        self.move(self.count, last, self.above)
+        self.move(1, self.first, self.stress(0, "vertical"))
 
 
 def pack_x(qf, qc, low, high):
@@ -252,7 +263,7 @@
 def kernel(
     fine_now, fine_before, fine_material, coarse_now, coarse_before, coarse_material,
     fine_out, coarse_out,
-    qf, qc, u1f, u1c, zf, zc,
+    qf, qc, u1f, u1c,
     sx_low, sx_high, sy, rx_low, rx_high, ry, rc,
     give, got, lanes_down, lanes_up, rows_down, rows_up,
     load_sem, send_sem, recv_sem, deep_send, deep_recv,
@@ -373,9 +384,26 @@
     unpack_x(qf, qc, rx_low, rx_high)
     unpack_y(qf, qc, ry, rc)
 
-    def deep_exchange(phase, cur_f, cur_c):
-        mine_f, theirs_f = jnp.where(top, FL, 1), jnp.where(top, 0, FL + 1)
-        mine_c, theirs_c = jnp.where(top, CL, 1), jnp.where(top, 0, CL + 1)
+    mine_f, theirs_f = jnp.where(top, FL, 1), jnp.where(top, 0, FL + 1)
+    mine_c, theirs_c = jnp.where(top, CL, 1), jnp.where(top, 0, CL + 1)
+
+    def deep_copy(src, dst, phase, k):
+        return pltpu.make_async_remote_copy(
+            src, dst, deep_send.at[phase, k], deep_recv.at[phase, k], device_id=partner, device_id_type=MESH
+        )
+
+    def deep_fine(phase, cur):
+        copy = deep_copy(cur.at[pl.ds(0, 3), mine_f], cur.at[pl.ds(0, 3), theirs_f], phase, 0)
+        copy.start()
+        return copy
+
+    def deep_coarse(phase, cur):
+        copy = deep_copy(cur.at[pl.ds(0, 3), mine_c], cur.at[pl.ds(0, 3), theirs_c], phase, 1)
+        copy.start()
+        return copy
+
+    def deep_interface(phase, cur_f, cur_c):
+        copy = deep_copy(give.at[phase], got.at[phase], phase, 2)
 
         @pl.when(top)
         def _():
@@ -389,38 +417,10 @@
             for c in range(3):
                 give[phase, c] = small[c * CR : (c + 1) * CR]
 
-        moves = [
-            (cur_f.at[pl.ds(0, 3), mine_f], cur_f.at[pl.ds(0, 3), theirs_f]),
-            (cur_c.at[pl.ds(0, 3), mine_c], cur_c.at[pl.ds(0, 3), theirs_c]),
-            (give.at[phase], got.at[phase]),
-        ]
-        copies = [
-            pltpu.make_async_remote_copy(
-                src, dst, deep_send.at[phase, k], deep_recv.at[phase, k], device_id=partner, device_id_type=MESH
-            )
-            for k, (src, dst) in enumerate(moves)
-        ]
-        for copy in copies:
-            copy.start()
-        if phase == 0:
-            medium = [
-                pltpu.make_async_remote_copy(
-                    src, dst, deep_send.at[0, 3 + k], deep_recv.at[0, 3 + k], device_id=partner, device_id_type=MESH
-                )
-                for k, (src, dst) in enumerate(
-                    (
-                        (qf.at[pl.ds(3, 3), FL], qf.at[pl.ds(3, 3), 0]),
-                        (qc.at[pl.ds(3, 2), CL], qc.at[pl.ds(3, 2), 0]),
-                    )
-                )
-            ]
-
-            @pl.when(top)
-            def _():
-                for copy in medium:
-                    copy.start()
-                for k in range(3, 5):
-                    qc[k, 0] = qc[k, 1]
+        copy.start()
+        return copy
+
+    def deep_arrived(phase, copies, cur_f, cur_c):
         for copy in copies:
             copy.wait_recv()
 
@@ -436,40 +436,63 @@
             for c in range(3):
                 cur_f[c, FL + 1] = large[c * FR : (c + 1) * FR]
 
-        for copy in copies:
-            copy.wait_send()
-        if phase == 0:
-            @pl.when(top)
-            def _():
-                for copy in medium:
-                    copy.wait_send()
-
-            @pl.when(jnp.logical_not(top))
-            def _():
-                for copy in medium:
-                    copy.wait_recv()
-
-    deep_exchange(0, qf, qc)
-
     def keep_f(c, slot, value):
         u1f[c, slot] = value
 
     def keep_c(c, slot, value):
         u1c[c, slot] = value
 
-    step(FL, qf, qf, lambda c, s: qf[6 + c, s], 9, True, zf, keep_f, (0, 0))
-    step(CL, qc, qc, lambda c, s: qc[5 + c, s], 8, False, zc, keep_c, (0, 0))
-
-    deep_exchange(1, u1f, u1c)
-
     def out_f(c, slot, value):
         fine_out[c, slot - 1] = value
 
     def out_c(c, slot, value):
         coarse_out[c, slot - 1] = value
 
-    step(FL, u1f, qf, lambda c, s: qf[c, s], 9, True, zf, out_f, (8, 128))
-    step(CL, u1c, qc, lambda c, s: qc[c, s], 8, False, zc, out_c, (8, 128))
+    first_f = Step(FL, qf, qf, lambda c, s: qf[6 + c, s], 9, True, keep_f, (0, 0))
+    first_c = Step(CL, qc, qc, lambda c, s: qc[5 + c, s], 8, False, keep_c, (0, 0))
+    second_f = Step(FL, u1f, qf, lambda c, s: qf[c, s], 9, True, out_f, (8, 128))
+    second_c = Step(CL, u1c, qc, lambda c, s: qc[c, s], 8, False, out_c, (8, 128))
+
+    deep = [deep_fine(0, qf), deep_coarse(0, qc)]
+    medium = [
+        deep_copy(qf.at[pl.ds(3, 3), FL], qf.at[pl.ds(3, 3), 0], 0, 3),
+        deep_copy(qc.at[pl.ds(3, 2), CL], qc.at[pl.ds(3, 2), 0], 0, 4),
+    ]
+
+    @pl.when(top)
+    def _():
+        for copy in medium:
+            copy.start()
+        for k in range(3, 5):
+            qc[k, 0] = qc[k, 1]
+
+    deep.append(deep_interface(0, qf, qc))
+    first_f.inner()
+    first_c.inner()
+    deep_arrived(0, deep, qf, qc)
+
+    @pl.when(jnp.logical_not(top))
+    def _():
+        for copy in medium:
+            copy.wait_recv()
+
+    first_f.outer()
+    later = [deep_fine(1, u1f)]
+    first_c.outer()
+    later += [deep_coarse(1, u1c), deep_interface(1, u1f, u1c)]
+    second_f.inner()
+    second_c.inner()
+    deep_arrived(1, later, u1f, u1c)
+    second_f.outer()
+    second_c.outer()
+
+    for copy in deep + later:
+        copy.wait_send()
+
+    @pl.when(top)
+    def _():
+        for copy in medium:
+            copy.wait_send()
 
     for k, copy in enumerate(sends):
         @pl.when(there[k][1])
@@ -481,7 +504,7 @@
     fine, coarse = arrays[0], arrays[3]
     return pl.pallas_call(
         kernel,
-        out_shape=(jax.ShapeDtypeStruct(fine.shape, F32), jax.ShapeDtypeStruct(coarse.shape, F32)),
+        out_shape=(pltpu.VMEM(fine.shape, F32), pltpu.VMEM(coarse.shape, F32)),
         in_specs=[pl.BlockSpec(memory_space=pltpu.HBM)] * 6,
         out_specs=(pl.BlockSpec(memory_space=pltpu.VMEM), pl.BlockSpec(memory_space=pltpu.VMEM)),
         scratch_shapes=[
@@ -489,8 +512,6 @@
             pltpu.VMEM((CQ, CL + 2, CR, CW), F32),
             pltpu.VMEM((3, FL + 2, FR, FW), F32),
             pltpu.VMEM((3, CL + 2, CR, CW), F32),
-            pltpu.VMEM((3, FR, FW), F32),
-            pltpu.VMEM((3, CR, CW), F32),
             pltpu.VMEM((X_LOW_ROWS, 128), F32),
             pltpu.VMEM((X_ROWS, 128), F32),
             pltpu.VMEM((Y_ROWS + C_FINE, 128), F32),
@@ -513,7 +534,7 @@
         compiler_params=pltpu.CompilerParams(
             collective_id=0, has_side_effects=True, vmem_limit_bytes=40 * 2**20
         ),
-    )(*arrays)
+    )(*[pltpu.with_memory_space_constraint(a, pltpu.HBM) for a in arrays])
 
 
 def solution(mesh):

time: 30.3 us -> 21 us (0.69)
  local copies, waits for them, and re-layouts: 6.79 us -> 1.32 us
  Pallas kernels: 22.6 us -> 18.9 us
    unnamed x14 -> x2, local copies, waits for them, and re-layouts: 6.79 us -> 1.32 us
    pallas_call x1, Pallas kernels: 22.6 us -> 18.9 us  [per_device(): pl.pallas_call(kernel, out_shape=(pltpu.VMEM(fine.shape, F32), pltpu.VMEM...]
where the time goes in v2:
time: 21 us; the launch traced here: 20.9 us
  Pallas kernels  18.9 us (90%)
  local copies, waits for them, and re-layouts  1.32 us (6%)
  between operations  0.64 us (3%)
    pallas_call x1, Pallas kernels, per_device(): pl.pallas_call(kernel, out_shape=(pltpu.VMEM(fine.shape, F32), pltpu.VMEM...  18.9 us
    unnamed x2, local copies, waits for them, and re-layouts  1.32 us

profile of v2, /device:TPU:249, one launch (start us, length us, event | category | flops | bytes accessed | tf_op | source)
XLA Modules:
  0.0 20.9 jit_solution(11380306974114722037)
XLA Ops:
  0.6 18.9 %shard_map.77 = (f32[3,4,16,256]{3,2,1,0:T(8,128)S(1)}, f32[3,8,8,128]{3,2,1,0:T(8,128)S(1)}) custom-call(f32[3,4,16,256]{3,2,1,0:T(8,128)} %fine_now.1, f32[3,4,16,256]{3,2,1,0:T(8,128)} %fine_before.1, f32[4,4,16,256]{3,2,1,0:T(8,128)} %fine_material.1, f32[3,8,8,128]{3,2,1,0:T(8,128)} %coarse_now.1, f32[3,8,8,128]{3,2,1,0:T(8,128)} %coarse_before.1, ...), custom_call_target="tpu_custom_call" | custom-call | tf_op jit(solution)/shard_map/pallas_call | solution.py:505
  19.5 0.7 %copy.10 = f32[3,4,16,256]{3,2,1,0:T(8,128)} copy(f32[3,4,16,256]{3,2,1,0:T(8,128)S(1)} %get-tuple-element.2) | data formatting | bytes 393216
  20.2 0.6 %copy.11 = f32[3,8,8,128]{3,2,1,0:T(8,128)} copy(f32[3,8,8,128]{3,2,1,0:T(8,128)S(1)} %get-tuple-element.3) | data formatting | bytes 196608

commit v3 on v2

--- a/solution.py
+++ b/solution.py
@@ -9,7 +9,6 @@
 STEP_SQUARED = 0.15 * 0.15
 MESH = pl.DeviceIdType.MESH
 F32 = jnp.float32
-BF16 = jnp.bfloat16
 
 FR, FW = 24, 384
 CR, CW = 16, 256
@@ -39,24 +38,43 @@
     return pltpu.roll(value, shift, axis) if shift else value
 
 
-def parts(value):
-    high = value.astype(BF16)
-    rest = value - high.astype(F32)
-    middle = rest.astype(BF16)
-    return high, middle, (rest - middle.astype(F32)).astype(BF16)
-
-
-def times_right(value, matrix):
-    return sum(jnp.dot(part, matrix, preferred_element_type=F32) for part in parts(value))
-
-
-def times_left(matrix, value):
-    return sum(jnp.dot(matrix, part, preferred_element_type=F32) for part in parts(value))
-
-
-def coarse_place(fine, half):
-    halo = jnp.where(fine < half, fine // 2, fine // 2 + half)
-    return jnp.where(fine < 2 * half, halo, fine // 2 + half)
+def picked(tile, index, axis):
+    return jnp.take_along_axis(tile, index, axis=axis)
+
+
+def restrict(tiles):
+    row, lane = iota((8, 128), 0), iota((8, 128), 1)
+    row_at, lane_at = (2 * row) & 7, (2 * lane) & 127
+
+    def pairs(tile, axis, at):
+        return picked(tile + turned(tile, -1, axis), at, axis)
+
+    def joined(halo, first, second, half, at):
+        return halo, jnp.where(at < half, first, second)
+
+    columns = []
+    for w in range(3):
+        columns.append(joined(*[pairs(tiles(r, w), 0, row_at) for r in range(3)], 4, row))
+    out = []
+    for r in range(2):
+        out.append(joined(*[0.25 * pairs(columns[w][r], 1, lane_at) for w in range(3)], 64, lane))
+    return out
+
+
+def prolong(tiles):
+    row, lane = iota((8, 128), 0), iota((8, 128), 1)
+
+    def spread(halo, own, half, at, axis):
+        low = at // 2
+        return (
+            picked(halo, jnp.where(at < half, low, low + half), axis),
+            picked(own, low, axis),
+            picked(own, low + half, axis),
+        )
+
+    rows = [spread(tiles(r, 0), tiles(r, 1), 64, lane, 1) for r in range(2)]
+    columns = [spread(rows[0][w], rows[1][w], 4, row, 0) for w in range(3)]
+    return [[columns[w][r] for w in range(3)] for r in range(3)]
 
 
 def gradients_to_stress(here, below, medium, stretch, which):
@@ -265,7 +283,7 @@
     fine_out, coarse_out,
     qf, qc, u1f, u1c,
     sx_low, sx_high, sy, rx_low, rx_high, ry, rc,
-    give, got, lanes_down, lanes_up, rows_down, rows_up,
+    give, got,
     load_sem, send_sem, recv_sem, deep_send, deep_recv,
 ):
     gx, gy, dev = lax.axis_index("gx"), lax.axis_index("gy"), lax.axis_index("dev")
@@ -330,18 +348,6 @@
         for c in range(3):
             qc[c, CL + 1] = jnp.zeros((CR, CW), F32)
             u1c[c, CL + 1] = jnp.zeros((CR, CW), F32)
-        place = coarse_place(iota((FW, CW), 0), 64)
-        lanes_down[...] = jnp.where(place == iota((FW, CW), 1), 0.5, 0.0).astype(BF16)
-        place = coarse_place(iota((CW, FW), 1), 64)
-        lanes_up[...] = jnp.where(place == iota((CW, FW), 0), 1.0, 0.0).astype(BF16)
-
-        def rows(shape, fine_dim):
-            fine, coarse = iota(shape, fine_dim), iota(shape, 1 - fine_dim)
-            place = coarse_place(fine % FR, 4)
-            return (place == coarse % CR) & (fine // FR == coarse // CR)
-
-        rows_down[...] = jnp.where(rows((3 * CR, 3 * FR), 1), 0.5, 0.0).astype(BF16)
-        rows_up[...] = jnp.where(rows((3 * FR, 3 * CR), 0), 1.0, 0.0).astype(BF16)
 
     for copy in copies:
         copy.wait()
@@ -412,10 +418,11 @@
 
         @pl.when(jnp.logical_not(top))
         def _():
-            fine = jnp.concatenate([cur_f[c, FL] for c in range(3)], axis=0)
-            small = times_left(rows_down[...], times_right(fine, lanes_down[...]))
             for c in range(3):
-                give[phase, c] = small[c * CR : (c + 1) * CR]
+                small = restrict(lambda r, w: cur_f[c, FL, 8 * r : 8 * r + 8, 128 * w : 128 * w + 128])
+                for r in range(2):
+                    for w in range(2):
+                        give[phase, c, 8 * r : 8 * r + 8, 128 * w : 128 * w + 128] = small[r][w]
 
         copy.start()
         return copy
@@ -431,10 +438,11 @@
 
         @pl.when(jnp.logical_not(top))
         def _():
-            coarse = jnp.concatenate([got[phase, c] for c in range(3)], axis=0)
-            large = times_left(rows_up[...], times_right(coarse, lanes_up[...]))
             for c in range(3):
-                cur_f[c, FL + 1] = large[c * FR : (c + 1) * FR]
+                large = prolong(lambda r, w: got[phase, c, 8 * r : 8 * r + 8, 128 * w : 128 * w + 128])
+                for r in range(3):
+                    for w in range(3):
+                        cur_f[c, FL + 1, 8 * r : 8 * r + 8, 128 * w : 128 * w + 128] = large[r][w]
 
     def keep_f(c, slot, value):
         u1f[c, slot] = value
@@ -500,8 +508,27 @@
             copy.wait_send()
 
 
+def store(fine, coarse, fine_out, coarse_out, sems):
+    copies = [pltpu.make_async_copy(fine, fine_out, sems.at[0]), pltpu.make_async_copy(coarse, coarse_out, sems.at[1])]
+    for copy in copies:
+        copy.start()
+    for copy in copies:
+        copy.wait()
+
+
 def per_device(*arrays):
     fine, coarse = arrays[0], arrays[3]
+    after = stepped(arrays, fine, coarse)
+    return pl.pallas_call(
+        store,
+        out_shape=(jax.ShapeDtypeStruct(fine.shape, F32), jax.ShapeDtypeStruct(coarse.shape, F32)),
+        in_specs=[pl.BlockSpec(memory_space=pltpu.VMEM)] * 2,
+        out_specs=(pl.BlockSpec(memory_space=pltpu.HBM), pl.BlockSpec(memory_space=pltpu.HBM)),
+        scratch_shapes=[pltpu.SemaphoreType.DMA((2,))],
+    )(*[pltpu.with_memory_space_constraint(a, pltpu.VMEM) for a in after])
+
+
+def stepped(arrays, fine, coarse):
     return pl.pallas_call(
         kernel,
         out_shape=(pltpu.VMEM(fine.shape, F32), pltpu.VMEM(coarse.shape, F32)),
@@ -521,10 +548,6 @@
             pltpu.VMEM((4, C_ROWS, 128), F32),
             pltpu.VMEM((STEPS, 3, CR, CW), F32),
             pltpu.VMEM((STEPS, 3, CR, CW), F32),
-            pltpu.VMEM((FW, CW), BF16),
-            pltpu.VMEM((CW, FW), BF16),
-            pltpu.VMEM((3 * CR, 3 * FR), BF16),
-            pltpu.VMEM((3 * FR, 3 * CR), BF16),
             pltpu.SemaphoreType.DMA((8,)),
             pltpu.SemaphoreType.DMA((8,)),
             pltpu.SemaphoreType.DMA((8,)),

time: 21 us -> 19.5 us (0.929)
  local copies, waits for them, and re-layouts: 1.32 us -> 0 us
    unnamed x2 -> x0, local copies, waits for them, and re-layouts: 1.32 us -> none
    pallas_call x1 -> x2, Pallas kernels: 18.9 us -> 18.7 us  [the longest x1 18 us: stepped(): pl.pallas_call(kernel, out_shape=(pltpu.VMEM(fine.shape, F32), pltpu.VMEM...]
where the time goes in v3:
time: 19.5 us; the launch traced here: 19.4 us
  Pallas kernels  18.7 us (96%)
  between operations  0.64 us (3%)
    pallas_call x1, Pallas kernels, stepped(): pl.pallas_call(kernel, out_shape=(pltpu.VMEM(fine.shape, F32), pltpu.VMEM...  18 us
    pallas_call x1, Pallas kernels, per_device(): pl.pallas_call(store, out_shape=(jax.ShapeDtypeStruct(fine.shape, F32), j...  0.72 us

profile of v3, /device:TPU:249, one launch (start us, length us, event | category | flops | bytes accessed | tf_op | source)
XLA Modules:
  0.0 19.4 jit_solution(740587789682491326)
XLA Ops:
  0.6 18.0 %shard_map.77 = (f32[3,4,16,256]{3,2,1,0:T(8,128)S(1)}, f32[3,8,8,128]{3,2,1,0:T(8,128)S(1)}) custom-call(f32[3,4,16,256]{3,2,1,0:T(8,128)} %fine_now.1, f32[3,4,16,256]{3,2,1,0:T(8,128)} %fine_before.1, f32[4,4,16,256]{3,2,1,0:T(8,128)} %fine_material.1, f32[3,8,8,128]{3,2,1,0:T(8,128)} %coarse_now.1, f32[3,8,8,128]{3,2,1,0:T(8,128)} %coarse_before.1, ...), custom_call_target="tpu_custom_call" | custom-call | tf_op jit(solution)/shard_map/pallas_call | solution.py:532
  18.7 0.7 %shard_map.78 = (f32[3,4,16,256]{3,2,1,0:T(8,128)}, f32[3,8,8,128]{3,2,1,0:T(8,128)}) custom-call(f32[3,4,16,256]{3,2,1,0:T(8,128)S(1)} %get-tuple-element.4.fine, f32[3,8,8,128]{3,2,1,0:T(8,128)S(1)} %get-tuple-element.5.coarse), custom_call_target="tpu_custom_call" | custom-call | tf_op jit(solution)/shard_map/pallas_call | solution.py:522

commit v4 on v3

--- a/solution.py
+++ b/solution.py
@@ -16,11 +16,13 @@
 FQ = 10
 CQ = 9
 
-X_FINE = FQ * 16
-X_COARSE = 14 * 8
-X_EXTRA = 3 * 16
-X_ROWS = X_FINE + X_COARSE + X_EXTRA
-X_LOW_ROWS = X_FINE + X_COARSE
+X_COARSE = 6 * 16
+X_EXTRA = X_COARSE + 10 * 8
+X_LOW_FIRST = X_EXTRA
+X_HIGH_FIRST = X_EXTRA + 3 * 16
+X_REST = 4 * 16 + 4 * 8
+X_LOW_ROWS = X_LOW_FIRST + X_REST
+X_ROWS = X_HIGH_FIRST + X_REST
 Y_FINE = 32
 Y_COARSE = 24
 C_FINE = 16
@@ -42,23 +44,19 @@
     return jnp.take_along_axis(tile, index, axis=axis)
 
 
-def restrict(tiles):
+def restrict(tiles, r, w):
     row, lane = iota((8, 128), 0), iota((8, 128), 1)
     row_at, lane_at = (2 * row) & 7, (2 * lane) & 127
 
     def pairs(tile, axis, at):
         return picked(tile + turned(tile, -1, axis), at, axis)
 
-    def joined(halo, first, second, half, at):
-        return halo, jnp.where(at < half, first, second)
-
-    columns = []
-    for w in range(3):
-        columns.append(joined(*[pairs(tiles(r, w), 0, row_at) for r in range(3)], 4, row))
-    out = []
-    for r in range(2):
-        out.append(joined(*[0.25 * pairs(columns[w][r], 1, lane_at) for w in range(3)], 64, lane))
-    return out
+    def joined(values, half, at):
+        return values[0] if len(values) == 1 else jnp.where(at < half, values[0], values[1])
+
+    sources = ((0,), (1, 2))
+    columns = [joined([pairs(tiles(a, b), 0, row_at) for a in sources[r]], 4, row) for b in sources[w]]
+    return joined([0.25 * pairs(v, 1, lane_at) for v in columns], 64, lane)
 
 
 def prolong(tiles):
@@ -154,6 +152,10 @@
         self.move(1, self.first, self.stress(0, "vertical"))
 
 
+def fine_at(g, first):
+    return g * 16 if g < 6 else first + (g - 6) * 16
+
+
 def pack_x(qf, qc, low, high):
     row8 = iota((8, 256), 0)
     crow = iota((8, 128), 0)
@@ -170,15 +172,15 @@
             t = turned(z, 2 * l, 0)
             up = t if l == 0 else jnp.where(row8 // 2 == l, t, up)
             down = t if l == 0 else jnp.where(row8 // 2 == l - 1, t, down)
-        store(high, g * 16, up)
-        store(low, g * 16, down)
+        store(high, fine_at(g, X_HIGH_FIRST), up)
+        store(low, fine_at(g, X_LOW_FIRST), down)
     for q in range(5):
         for half in range(2):
             for l in range(4):
                 t = turned(qc[q, half * 4 + l + 1, 8:16, 128:], 2 * l, 0)
                 up = t if l == 0 else jnp.where(crow // 2 == l, t, up)
                 down = t if l == 0 else jnp.where(crow // 2 == l - 1, t, down)
-            at = X_FINE + (q * 2 + half) * 8
+            at = X_COARSE + (q * 2 + half) * 8
             high[pl.ds(at, 8), :] = up
             low[pl.ds(at, 8), :] = down
     for q in range(4):
@@ -186,25 +188,24 @@
             t = turned(qc[5 + q, l + 1, 8:16, 128:], l, 0)
             up = t if l == 0 else jnp.where(crow == l, t, up)
             down = t if l == 0 else jnp.where(crow == l - 1, t, down)
-        at = X_FINE + (10 + q) * 8
-        high[pl.ds(at, 8), :] = up
-        low[pl.ds(at, 8), :] = down
+        high[pl.ds(X_HIGH_FIRST + 64 + q * 8, 8), :] = up
+        low[pl.ds(X_LOW_FIRST + 64 + q * 8, 8), :] = down
     for c in range(3):
         more = jnp.where(row8 < 2, turned(qf[c, 3, 8:16, 128:], -2, 0), qf[c, 4, 8:16, 128:])
-        store(high, X_FINE + X_COARSE + c * 16, more)
-
-
-def unpack_x(qf, qc, low, high):
+        store(high, X_EXTRA + c * 16, more)
+
+
+def unpack_x(qf, qc, low, high, first):
     row8 = iota((8, 256), 0)
     crow = iota((8, 128), 0)
 
     def load(ref, at):
         return jnp.concatenate([ref[pl.ds(at, 8), :], ref[pl.ds(at + 8, 8), :]], axis=1)
 
-    for g in range(FQ):
-        up = load(high, g * 16)
-        down = load(low, g * 16)
-        more = load(high, X_FINE + X_COARSE + g * 16) if g < 3 else None
+    for g in range(6) if first else range(6, FQ):
+        up = load(high, fine_at(g, X_HIGH_FIRST))
+        down = load(low, fine_at(g, X_LOW_FIRST))
+        more = load(high, X_EXTRA + g * 16) if g < 3 else None
         for l in range(FL):
             t = jnp.where(row8 < 4, turned(up, -2 * l, 0), turned(down, -2 * l, 0))
             if g < 3 and l == 2:
@@ -212,18 +213,17 @@
             if g < 3 and l == 3:
                 t = jnp.where(row8 // 2 == 1, more, t)
             qf[g, l + 1, 0:8, 128:] = t
-    for q in range(5):
+    for q in range(5) if first else ():
         for half in range(2):
-            at = X_FINE + (q * 2 + half) * 8
+            at = X_COARSE + (q * 2 + half) * 8
             up = high[pl.ds(at, 8), :]
             down = low[pl.ds(at, 8), :]
             for l in range(4):
                 t = jnp.where(crow < 4, turned(up, -2 * l, 0), turned(down, -2 * l, 0))
                 qc[q, half * 4 + l + 1, 0:8, 128:] = t
-    for q in range(4):
-        at = X_FINE + (10 + q) * 8
-        up = high[pl.ds(at, 8), :]
-        down = low[pl.ds(at, 8), :]
+    for q in () if first else range(4):
+        up = high[pl.ds(X_HIGH_FIRST + 64 + q * 8, 8), :]
+        down = low[pl.ds(X_LOW_FIRST + 64 + q * 8, 8), :]
         for l in range(8):
             qc[5 + q, l + 1, 0:8, 128:] = jnp.where(crow < 4, turned(up, -l, 0), turned(down, -l, 0))
 
@@ -359,90 +359,112 @@
         qc[own] = (0.25 * STEP_SQUARED) / qc[own]
     pack_x(qf, qc, sx_low, sx_high)
     pack_y(qf, qc, sy)
-    pl.semaphore_wait(barrier, expected)
-
-    side_msg, corner_msg = sy.at[pl.ds(0, Y_ROWS)], sy.at[pl.ds(Y_FINE, C_ROWS)]
-    messages = [
-        (sx_high, rx_high), (sx_low, rx_low), (side_msg, ry.at[1]), (side_msg, ry.at[0]),
-        (corner_msg, rc.at[3]), (corner_msg, rc.at[2]), (corner_msg, rc.at[1]), (corner_msg, rc.at[0]),
-    ]
-    sends = []
-    for k, (src, dst) in enumerate(messages):
-        copy = pltpu.make_async_remote_copy(
-            src, dst, send_sem.at[k], recv_sem.at[k], device_id=there[k][0], device_id_type=MESH
-        )
-
-        @pl.when(there[k][1])
-        def _(copy=copy):
-            copy.start()
-
-        sends.append(copy)
-
-    def arrived(k):
-        opposite = SIDES.index((-SIDES[k][0], -SIDES[k][1]))
-
-        @pl.when(there[opposite][1])
-        def _():
-            sends[k].wait_recv()
-
-    for k in range(8):
-        arrived(k)
-    unpack_x(qf, qc, rx_low, rx_high)
-    unpack_y(qf, qc, ry, rc)
-
-    mine_f, theirs_f = jnp.where(top, FL, 1), jnp.where(top, 0, FL + 1)
-    mine_c, theirs_c = jnp.where(top, CL, 1), jnp.where(top, 0, CL + 1)
+
+    areas = (
+        ((pl.ds(8, 16), pl.ds(128, 256)), (pl.ds(8, 8), pl.ds(128, 128)), ((1, 1),)),
+        ((pl.ds(0, FR), pl.ds(0, 128)), (pl.ds(0, CR), pl.ds(0, 128)), ((0, 0), (1, 0))),
+        ((pl.ds(0, 8), pl.ds(128, 256)), (pl.ds(0, 8), pl.ds(128, 128)), ((0, 1),)),
+    )
 
     def deep_copy(src, dst, phase, k):
         return pltpu.make_async_remote_copy(
             src, dst, deep_send.at[phase, k], deep_recv.at[phase, k], device_id=partner, device_id_type=MESH
         )
 
-    def deep_fine(phase, cur):
-        copy = deep_copy(cur.at[pl.ds(0, 3), mine_f], cur.at[pl.ds(0, 3), theirs_f], phase, 0)
-        copy.start()
-        return copy
-
-    def deep_coarse(phase, cur):
-        copy = deep_copy(cur.at[pl.ds(0, 3), mine_c], cur.at[pl.ds(0, 3), theirs_c], phase, 1)
-        copy.start()
-        return copy
-
-    def deep_interface(phase, cur_f, cur_c):
-        copy = deep_copy(give.at[phase], got.at[phase], phase, 2)
-
-        @pl.when(top)
-        def _():
-            for c in range(3):
-                give[phase, c] = cur_c[c, 1]
-
+    def restricted(phase, cur_f, places):
         @pl.when(jnp.logical_not(top))
         def _():
             for c in range(3):
-                small = restrict(lambda r, w: cur_f[c, FL, 8 * r : 8 * r + 8, 128 * w : 128 * w + 128])
-                for r in range(2):
-                    for w in range(2):
-                        give[phase, c, 8 * r : 8 * r + 8, 128 * w : 128 * w + 128] = small[r][w]
-
-        copy.start()
-        return copy
-
-    def deep_arrived(phase, copies, cur_f, cur_c):
-        for copy in copies:
-            copy.wait_recv()
-
+                for r, w in places:
+                    give[phase, c, 8 * r : 8 * r + 8, 128 * w : 128 * w + 128] = restrict(
+                        lambda a, b: cur_f[c, FL, 8 * a : 8 * a + 8, 128 * b : 128 * b + 128], r, w
+                    )
+
+    from_top, from_bottom = [], []
+    for part, (fine, coarse, _) in enumerate(areas):
+        from_top.append(
+            [
+                deep_copy(qf.at[(pl.ds(0, 6), FL, *fine)], qf.at[(pl.ds(0, 6), 0, *fine)], 0, part * 3),
+                deep_copy(qc.at[(pl.ds(0, 5), CL, *coarse)], qc.at[(pl.ds(0, 5), 0, *coarse)], 0, part * 3 + 1),
+                deep_copy(qc.at[(pl.ds(0, 3), 1, *coarse)], got.at[(0, pl.ds(0, 3), *coarse)], 0, part * 3 + 2),
+            ]
+        )
+        from_bottom.append(
+            [
+                deep_copy(qf.at[(pl.ds(0, 3), 1, *fine)], qf.at[(pl.ds(0, 3), FL + 1, *fine)], 0, part * 3),
+                deep_copy(qc.at[(pl.ds(0, 3), 1, *coarse)], qc.at[(pl.ds(0, 3), CL + 1, *coarse)], 0, part * 3 + 1),
+                deep_copy(give.at[(0, pl.ds(0, 3), *coarse)], qc.at[(pl.ds(0, 3), 0, *coarse)], 0, part * 3 + 2),
+            ]
+        )
+
+    def start_part(part):
         @pl.when(top)
         def _():
-            for c in range(3):
-                cur_c[c, 0] = got[phase, c]
+            for copy in from_top[part]:
+                copy.start()
 
         @pl.when(jnp.logical_not(top))
         def _():
-            for c in range(3):
-                large = prolong(lambda r, w: got[phase, c, 8 * r : 8 * r + 8, 128 * w : 128 * w + 128])
-                for r in range(3):
-                    for w in range(3):
-                        cur_f[c, FL + 1, 8 * r : 8 * r + 8, 128 * w : 128 * w + 128] = large[r][w]
+            for copy in from_bottom[part]:
+                copy.start()
+
+    restricted(0, qf, areas[0][2])
+    pl.semaphore_wait(barrier, expected)
+
+    side_msg, corner_msg = sy.at[pl.ds(0, Y_ROWS)], sy.at[pl.ds(Y_FINE, C_ROWS)]
+    high_first, high_rest = pl.ds(0, X_HIGH_FIRST), pl.ds(X_HIGH_FIRST, X_REST)
+    low_first, low_rest = pl.ds(0, X_LOW_FIRST), pl.ds(X_LOW_FIRST, X_REST)
+    messages = [
+        (4, corner_msg, rc.at[3]), (5, corner_msg, rc.at[2]), (6, corner_msg, rc.at[1]), (7, corner_msg, rc.at[0]),
+        (2, side_msg, ry.at[1]), (3, side_msg, ry.at[0]),
+        (0, sx_high.at[high_first], rx_high.at[high_first]), (1, sx_low.at[low_first], rx_low.at[low_first]),
+        (0, sx_high.at[high_rest], rx_high.at[high_rest]), (1, sx_low.at[low_rest], rx_low.at[low_rest]),
+    ]
+    sends = []
+    for n, (k, src, dst) in enumerate(messages):
+        copy = pltpu.make_async_remote_copy(
+            src, dst, send_sem.at[n], recv_sem.at[n], device_id=there[k][0], device_id_type=MESH
+        )
+
+        @pl.when(there[k][1])
+        def _(copy=copy):
+            copy.start()
+
+        sends.append((k, copy))
+
+    def arrived(*numbers):
+        for n in numbers:
+            k, copy = sends[n]
+            opposite = SIDES.index((-SIDES[k][0], -SIDES[k][1]))
+
+            @pl.when(there[opposite][1])
+            def _(copy=copy):
+                copy.wait_recv()
+
+    start_part(0)
+    arrived(0, 1, 2, 3, 4, 5)
+    unpack_y(qf, qc, ry, rc)
+    restricted(0, qf, areas[1][2])
+    start_part(1)
+    arrived(6, 7)
+    unpack_x(qf, qc, rx_low, rx_high, True)
+    restricted(0, qf, areas[2][2])
+    start_part(2)
+
+    @pl.when(top)
+    def _():
+        for k in range(3, 5):
+            qc[k, 0] = qc[k, 1]
+
+    arrived(8, 9)
+    unpack_x(qf, qc, rx_low, rx_high, False)
+
+    def prolonged(phase, cur_f):
+        for c in range(3):
+            large = prolong(lambda r, w: got[phase, c, 8 * r : 8 * r + 8, 128 * w : 128 * w + 128])
+            for r in range(3):
+                for w in range(3):
+                    cur_f[c, FL + 1, 8 * r : 8 * r + 8, 128 * w : 128 * w + 128] = large[r][w]
 
     def keep_f(c, slot, value):
         u1f[c, slot] = value
@@ -461,48 +483,75 @@
     second_f = Step(FL, u1f, qf, lambda c, s: qf[c, s], 9, True, out_f, (8, 128))
     second_c = Step(CL, u1c, qc, lambda c, s: qc[c, s], 8, False, out_c, (8, 128))
 
-    deep = [deep_fine(0, qf), deep_coarse(0, qc)]
-    medium = [
-        deep_copy(qf.at[pl.ds(3, 3), FL], qf.at[pl.ds(3, 3), 0], 0, 3),
-        deep_copy(qc.at[pl.ds(3, 2), CL], qc.at[pl.ds(3, 2), 0], 0, 4),
-    ]
-
-    @pl.when(top)
-    def _():
-        for copy in medium:
-            copy.start()
-        for k in range(3, 5):
-            qc[k, 0] = qc[k, 1]
-
-    deep.append(deep_interface(0, qf, qc))
     first_f.inner()
     first_c.inner()
-    deep_arrived(0, deep, qf, qc)
+
+    @pl.when(top)
+    def _():
+        for part in from_bottom:
+            for copy in part:
+                copy.wait_recv()
 
     @pl.when(jnp.logical_not(top))
     def _():
-        for copy in medium:
-            copy.wait_recv()
+        for part in from_top:
+            for copy in part:
+                copy.wait_recv()
+        prolonged(0, qf)
+
+    mine_f, theirs_f = jnp.where(top, FL, 1), jnp.where(top, 0, FL + 1)
+    mine_c, theirs_c = jnp.where(top, CL, 1), jnp.where(top, 0, CL + 1)
+    later_f = deep_copy(u1f.at[pl.ds(0, 3), mine_f], u1f.at[pl.ds(0, 3), theirs_f], 1, 0)
+    later_c = deep_copy(u1c.at[pl.ds(0, 3), mine_c], u1c.at[pl.ds(0, 3), theirs_c], 1, 1)
+    down = deep_copy(u1c.at[pl.ds(0, 3), 1], got.at[1], 1, 2)
+    up = deep_copy(give.at[1], u1c.at[pl.ds(0, 3), 0], 1, 2)
 
     first_f.outer()
-    later = [deep_fine(1, u1f)]
+    later_f.start()
+    restricted(1, u1f, ((0, 0), (0, 1), (1, 0), (1, 1)))
+
+    @pl.when(jnp.logical_not(top))
+    def _():
+        up.start()
+
     first_c.outer()
-    later += [deep_coarse(1, u1c), deep_interface(1, u1f, u1c)]
+    later_c.start()
+
+    @pl.when(top)
+    def _():
+        down.start()
+
     second_f.inner()
     second_c.inner()
-    deep_arrived(1, later, u1f, u1c)
+    later_f.wait_recv()
+    later_c.wait_recv()
+
+    @pl.when(top)
+    def _():
+        up.wait_recv()
+
+    @pl.when(jnp.logical_not(top))
+    def _():
+        down.wait_recv()
+        prolonged(1, u1f)
+
     second_f.outer()
     second_c.outer()
 
-    for copy in deep + later:
-        copy.wait_send()
+    later_f.wait_send()
+    later_c.wait_send()
 
     @pl.when(top)
     def _():
-        for copy in medium:
+        for copy in [copy for part in from_top for copy in part] + [down]:
             copy.wait_send()
 
-    for k, copy in enumerate(sends):
+    @pl.when(jnp.logical_not(top))
+    def _():
+        for copy in [copy for part in from_bottom for copy in part] + [up]:
+            copy.wait_send()
+
+    for k, copy in sends:
         @pl.when(there[k][1])
         def _(copy=copy):
             copy.wait_send()
@@ -549,10 +598,10 @@
             pltpu.VMEM((STEPS, 3, CR, CW), F32),
             pltpu.VMEM((STEPS, 3, CR, CW), F32),
             pltpu.SemaphoreType.DMA((8,)),
-            pltpu.SemaphoreType.DMA((8,)),
-            pltpu.SemaphoreType.DMA((8,)),
-            pltpu.SemaphoreType.DMA((STEPS, 5)),
-            pltpu.SemaphoreType.DMA((STEPS, 5)),
+            pltpu.SemaphoreType.DMA((10,)),
+            pltpu.SemaphoreType.DMA((10,)),
+            pltpu.SemaphoreType.DMA((STEPS, 9)),
+            pltpu.SemaphoreType.DMA((STEPS, 9)),
         ],
         compiler_params=pltpu.CompilerParams(
             collective_id=0, has_side_effects=True, vmem_limit_bytes=40 * 2**20

time: 19.5 us -> 18.8 us (0.964)
  the two profiles are of different devices: /device:TPU:249 before, /device:TPU:199 now
where the time goes in v4:
time: 18.8 us; the launch traced here: 18.7 us
  Pallas kernels  18 us (96%)
  between operations  0.64 us (3%)
    pallas_call x1, Pallas kernels, stepped(): pl.pallas_call(kernel, out_shape=(pltpu.VMEM(fine.shape, F32), pltpu.VMEM...  17.3 us
    pallas_call x1, Pallas kernels, per_device(): pl.pallas_call(store, out_shape=(jax.ShapeDtypeStruct(fine.shape, F32), j...  0.72 us

profile of v4, /device:TPU:199, one launch (start us, length us, event | category | flops | bytes accessed | tf_op | source)
XLA Modules:
  0.0 18.7 jit_solution(15493744550367279341)
XLA Ops:
  0.6 17.3 %shard_map.77 = (f32[3,4,16,256]{3,2,1,0:T(8,128)S(1)}, f32[3,8,8,128]{3,2,1,0:T(8,128)S(1)}) custom-call(f32[3,4,16,256]{3,2,1,0:T(8,128)} %fine_now.1, f32[3,4,16,256]{3,2,1,0:T(8,128)} %fine_before.1, f32[4,4,16,256]{3,2,1,0:T(8,128)} %fine_material.1, f32[3,8,8,128]{3,2,1,0:T(8,128)} %coarse_now.1, f32[3,8,8,128]{3,2,1,0:T(8,128)} %coarse_before.1, ...), custom_call_target="tpu_custom_call" | custom-call | tf_op jit(solution)/shard_map/pallas_call | solution.py:581
  18.0 0.7 %shard_map.78 = (f32[3,4,16,256]{3,2,1,0:T(8,128)}, f32[3,8,8,128]{3,2,1,0:T(8,128)}) custom-call(f32[3,4,16,256]{3,2,1,0:T(8,128)S(1)} %get-tuple-element.4.fine, f32[3,8,8,128]{3,2,1,0:T(8,128)S(1)} %get-tuple-element.5.coarse), custom_call_target="tpu_custom_call" | custom-call | tf_op jit(solution)/shard_map/pallas_call | solution.py:571

commit v5 on v4

--- a/solution.py
+++ b/solution.py
@@ -19,15 +19,14 @@
 X_COARSE = 6 * 16
 X_EXTRA = X_COARSE + 10 * 8
 X_LOW_FIRST = X_EXTRA
-X_HIGH_FIRST = X_EXTRA + 3 * 16
+X_HIGH_FIRST = X_EXTRA + 2 * 16
 X_REST = 4 * 16 + 4 * 8
 X_LOW_ROWS = X_LOW_FIRST + X_REST
 X_ROWS = X_HIGH_FIRST + X_REST
 Y_FINE = 32
 Y_COARSE = 24
-C_FINE = 16
 Y_ROWS = Y_FINE + Y_COARSE
-C_ROWS = Y_COARSE + C_FINE
+C_ROWS = 16
 SIDES = ((-1, 0), (1, 0), (0, -1), (0, 1), (-1, -1), (-1, 1), (1, -1), (1, 1))
 
 
@@ -190,9 +189,9 @@
             down = t if l == 0 else jnp.where(crow == l - 1, t, down)
         high[pl.ds(X_HIGH_FIRST + 64 + q * 8, 8), :] = up
         low[pl.ds(X_LOW_FIRST + 64 + q * 8, 8), :] = down
-    for c in range(3):
-        more = jnp.where(row8 < 2, turned(qf[c, 3, 8:16, 128:], -2, 0), qf[c, 4, 8:16, 128:])
-        store(high, X_EXTRA + c * 16, more)
+    more = [jnp.where(row8 < 2, turned(qf[c, 3, 8:16, 128:], -2, 0), qf[c, 4, 8:16, 128:]) for c in range(3)]
+    store(high, X_EXTRA, jnp.where(row8 < 4, more[0], turned(more[1], 4, 0)))
+    store(high, X_EXTRA + 16, more[2])
 
 
 def unpack_x(qf, qc, low, high, first):
@@ -205,7 +204,7 @@
     for g in range(6) if first else range(6, FQ):
         up = load(high, fine_at(g, X_HIGH_FIRST))
         down = load(low, fine_at(g, X_LOW_FIRST))
-        more = load(high, X_EXTRA + g * 16) if g < 3 else None
+        more = turned(load(high, X_EXTRA + g // 2 * 16), -4 * (g % 2), 0) if g < 3 else None
         for l in range(FL):
             t = jnp.where(row8 < 4, turned(up, -2 * l, 0), turned(down, -2 * l, 0))
             if g < 3 and l == 2:
@@ -228,10 +227,11 @@
             qc[5 + q, l + 1, 0:8, 128:] = jnp.where(crow < 4, turned(up, -l, 0), turned(down, -l, 0))
 
 
-def pack_y(qf, qc, out):
+def pack_y(qf, qc, out, corner):
     lane = iota((16, 128), 1)
     lane8 = iota((8, 128), 1)
     row8 = iota((8, 128), 0)
+    fine, coarse = [], []
     for t in range(2):
         packed = jnp.zeros((16, 128), F32)
         for k in range(20):
@@ -240,7 +240,7 @@
             mine = ((lane + (2 - 6 * k + 128)) & 127) < 6
             packed = jnp.where(mine, turned(z, 6 * k, 1), packed)
         out[pl.ds(t * 16, 16), :] = packed
-        out[pl.ds(Y_ROWS + t * 8, 8), :] = jnp.where(row8 < 4, packed[:8], packed[8:])
+        fine.append(packed)
     for t in range(3):
         packed = jnp.zeros((8, 128), F32)
         for k in range(32 if t < 2 else 8):
@@ -248,6 +248,15 @@
             mine = ((lane8 + (2 - 4 * k + 128)) & 127) < 4
             packed = jnp.where(mine, turned(qc[q, l + 1, 8:16, 128:256], 4 * k, 1), packed)
         out[pl.ds(Y_FINE + t * 8, 8), :] = packed
+        coarse.append(packed)
+    corner[0, 0:8] = jnp.where(row8 < 4, fine[0][:8], turned(fine[1][:8], 4, 0))
+    corner[0, 8:16] = jnp.where(
+        row8 < 2, coarse[0], jnp.where(row8 < 4, turned(coarse[1], 2, 0), turned(coarse[2], 4, 0))
+    )
+    corner[1, 0:8] = jnp.where(row8 >= 6, fine[0][8:], turned(fine[1][8:], -2, 0))
+    corner[1, 8:16] = jnp.where(
+        row8 >= 6, coarse[0], jnp.where(row8 >= 4, turned(coarse[1], -2, 0), turned(coarse[2], -4, 0))
+    )
 
 
 def unpack_y(qf, qc, side, corner):
@@ -258,21 +267,21 @@
     fine_low8 = ((lane8 + 2) & 127) % 6 < 2
     coarse_low8 = ((lane8 + 2) & 127) % 4 < 2
 
-    def corners(at, low):
-        before = jnp.where(low, corner[0, pl.ds(at, 8), :], corner[1, pl.ds(at, 8), :])
-        after = jnp.where(low, corner[2, pl.ds(at, 8), :], corner[3, pl.ds(at, 8), :])
-        return jnp.where(row8 < 4, after, before)
+    def corners(at, low, up, down):
+        before = jnp.where(low, corner[0, at : at + 8], corner[1, at : at + 8])
+        after = jnp.where(low, corner[2, at : at + 8], corner[3, at : at + 8])
+        return jnp.where(row8 < 4, turned(after, up, 0), turned(before, down, 0))
 
     for t in range(2):
         own = jnp.where(fine_low, side[0, pl.ds(t * 16, 16), :], side[1, pl.ds(t * 16, 16), :])
-        both = jnp.concatenate([corners(Y_COARSE + t * 8, fine_low8), own], axis=0)
+        both = jnp.concatenate([corners(0, fine_low8, -4 * t, 2 * t), own], axis=0)
         for k in range(20):
             g, l = t * 5 + k // 4, k % 4
             qf[g, l + 1, :, 0:128] = turned(both, -6 * k, 1)
     for t in range(3):
         at = Y_FINE + t * 8
         own = jnp.where(coarse_low8, side[0, pl.ds(at, 8), :], side[1, pl.ds(at, 8), :])
-        both = jnp.concatenate([corners(t * 8, coarse_low8), own], axis=0)
+        both = jnp.concatenate([corners(8, coarse_low8, -2 * t, 2 * t), own], axis=0)
         for k in range(32 if t < 2 else 8):
             q, l = t * 4 + k // 8, k % 8
             qc[q, l + 1, :, 0:128] = turned(both, -4 * k, 1)
@@ -282,7 +291,7 @@
     fine_now, fine_before, fine_material, coarse_now, coarse_before, coarse_material,
     fine_out, coarse_out,
     qf, qc, u1f, u1c,
-    sx_low, sx_high, sy, rx_low, rx_high, ry, rc,
+    sx_low, sx_high, sy, sc, rx_low, rx_high, ry, rc,
     give, got,
     load_sem, send_sem, recv_sem, deep_send, deep_recv,
 ):
@@ -358,7 +367,7 @@
         own = (8, l + 1, pl.ds(8, 8), pl.ds(128, 128))
         qc[own] = (0.25 * STEP_SQUARED) / qc[own]
     pack_x(qf, qc, sx_low, sx_high)
-    pack_y(qf, qc, sy)
+    pack_y(qf, qc, sy, sc)
 
     areas = (
         ((pl.ds(8, 16), pl.ds(128, 256)), (pl.ds(8, 8), pl.ds(128, 128)), ((1, 1),)),
@@ -411,13 +420,12 @@
     restricted(0, qf, areas[0][2])
     pl.semaphore_wait(barrier, expected)
 
-    side_msg, corner_msg = sy.at[pl.ds(0, Y_ROWS)], sy.at[pl.ds(Y_FINE, C_ROWS)]
     high_first, high_rest = pl.ds(0, X_HIGH_FIRST), pl.ds(X_HIGH_FIRST, X_REST)
     low_first, low_rest = pl.ds(0, X_LOW_FIRST), pl.ds(X_LOW_FIRST, X_REST)
     messages = [
-        (4, corner_msg, rc.at[3]), (5, corner_msg, rc.at[2]), (6, corner_msg, rc.at[1]), (7, corner_msg, rc.at[0]),
-        (2, side_msg, ry.at[1]), (3, side_msg, ry.at[0]),
         (0, sx_high.at[high_first], rx_high.at[high_first]), (1, sx_low.at[low_first], rx_low.at[low_first]),
+        (2, sy, ry.at[1]), (3, sy, ry.at[0]),
+        (4, sc.at[0], rc.at[3]), (5, sc.at[0], rc.at[2]), (6, sc.at[1], rc.at[1]), (7, sc.at[1], rc.at[0]),
         (0, sx_high.at[high_rest], rx_high.at[high_rest]), (1, sx_low.at[low_rest], rx_low.at[low_rest]),
     ]
     sends = []
@@ -442,11 +450,11 @@
                 copy.wait_recv()
 
     start_part(0)
-    arrived(0, 1, 2, 3, 4, 5)
+    arrived(2, 3, 4, 5, 6, 7)
     unpack_y(qf, qc, ry, rc)
     restricted(0, qf, areas[1][2])
     start_part(1)
-    arrived(6, 7)
+    arrived(0, 1)
     unpack_x(qf, qc, rx_low, rx_high, True)
     restricted(0, qf, areas[2][2])
     start_part(2)
@@ -590,7 +598,8 @@
             pltpu.VMEM((3, CL + 2, CR, CW), F32),
             pltpu.VMEM((X_LOW_ROWS, 128), F32),
             pltpu.VMEM((X_ROWS, 128), F32),
-            pltpu.VMEM((Y_ROWS + C_FINE, 128), F32),
+            pltpu.VMEM((Y_ROWS, 128), F32),
+            pltpu.VMEM((2, C_ROWS, 128), F32),
             pltpu.VMEM((X_LOW_ROWS, 128), F32),
             pltpu.VMEM((X_ROWS, 128), F32),
             pltpu.VMEM((2, Y_ROWS, 128), F32),

time: 18.8 us -> 18.4 us (0.979)
  the two profiles are of different devices: /device:TPU:199 before, /device:TPU:1 now
where the time goes in v5:
time: 18.4 us; the launch traced here: 18.3 us
  Pallas kernels  17.6 us (96%)
  between operations  0.64 us (3%)
    pallas_call x1, Pallas kernels, stepped(): pl.pallas_call(kernel, out_shape=(pltpu.VMEM(fine.shape, F32), pltpu.VMEM...  16.9 us
    pallas_call x1, Pallas kernels, per_device(): pl.pallas_call(store, out_shape=(jax.ShapeDtypeStruct(fine.shape, F32), j...  0.72 us

profile of v5, /device:TPU:1, one launch (start us, length us, event | category | flops | bytes accessed | tf_op | source)
XLA Modules:
  0.0 18.3 jit_solution(14527039463840537670)
XLA Ops:
  0.6 16.9 %shard_map.77 = (f32[3,4,16,256]{3,2,1,0:T(8,128)S(1)}, f32[3,8,8,128]{3,2,1,0:T(8,128)S(1)}) custom-call(f32[3,4,16,256]{3,2,1,0:T(8,128)} %fine_now.1, f32[3,4,16,256]{3,2,1,0:T(8,128)} %fine_before.1, f32[4,4,16,256]{3,2,1,0:T(8,128)} %fine_material.1, f32[3,8,8,128]{3,2,1,0:T(8,128)} %coarse_now.1, f32[3,8,8,128]{3,2,1,0:T(8,128)} %coarse_before.1, ...), custom_call_target="tpu_custom_call" | custom-call | tf_op jit(solution)/shard_map/pallas_call | solution.py:589
  17.6 0.7 %shard_map.78 = (f32[3,4,16,256]{3,2,1,0:T(8,128)}, f32[3,8,8,128]{3,2,1,0:T(8,128)}) custom-call(f32[3,4,16,256]{3,2,1,0:T(8,128)S(1)} %get-tuple-element.4.fine, f32[3,8,8,128]{3,2,1,0:T(8,128)S(1)} %get-tuple-element.5.coarse), custom_call_target="tpu_custom_call" | custom-call | tf_op jit(solution)/shard_map/pallas_call | solution.py:579

commit v6 on v5

--- a/solution.py
+++ b/solution.py
@@ -17,8 +17,9 @@
 CQ = 9
 
 X_COARSE = 6 * 16
-X_EXTRA = X_COARSE + 10 * 8
-X_LOW_FIRST = X_EXTRA
+X_MEDIUM = X_COARSE + 6 * 8
+X_EXTRA = X_MEDIUM + 2 * 8
+X_LOW_FIRST = X_COARSE + 10 * 8
 X_HIGH_FIRST = X_EXTRA + 2 * 16
 X_REST = 4 * 16 + 4 * 8
 X_LOW_ROWS = X_LOW_FIRST + X_REST
@@ -180,8 +181,14 @@
                 up = t if l == 0 else jnp.where(crow // 2 == l, t, up)
                 down = t if l == 0 else jnp.where(crow // 2 == l - 1, t, down)
             at = X_COARSE + (q * 2 + half) * 8
-            high[pl.ds(at, 8), :] = up
+            if q < 3:
+                high[pl.ds(at, 8), :] = up
             low[pl.ds(at, 8), :] = down
+    for q in range(3, 5):
+        for l in range(8):
+            t = turned(qc[q, l + 1, 8:16, 128:], l, 0)
+            up = t if l == 0 else jnp.where(crow == l, t, up)
+        high[pl.ds(X_MEDIUM + (q - 3) * 8, 8), :] = up
     for q in range(4):
         for l in range(8):
             t = turned(qc[5 + q, l + 1, 8:16, 128:], l, 0)
@@ -215,10 +222,11 @@
     for q in range(5) if first else ():
         for half in range(2):
             at = X_COARSE + (q * 2 + half) * 8
-            up = high[pl.ds(at, 8), :]
+            up = high[pl.ds(at if q < 3 else X_MEDIUM + (q - 3) * 8, 8), :]
             down = low[pl.ds(at, 8), :]
             for l in range(4):
-                t = jnp.where(crow < 4, turned(up, -2 * l, 0), turned(down, -2 * l, 0))
+                shift = 2 * l if q < 3 else half * 4 + l
+                t = jnp.where(crow < 4, turned(up, -shift, 0), turned(down, -2 * l, 0))
                 qc[q, half * 4 + l + 1, 0:8, 128:] = t
     for q in () if first else range(4):
         up = high[pl.ds(X_HIGH_FIRST + 64 + q * 8, 8), :]

time: 18.4 us -> 18.3 us (level)
  no operation moved by 1% of the time
where the time goes in v6:
time: 18.3 us; the launch traced here: 18.2 us
  Pallas kernels  17.6 us (96%)
  between operations  0.64 us (3%)
    pallas_call x1, Pallas kernels, stepped(): pl.pallas_call(kernel, out_shape=(pltpu.VMEM(fine.shape, F32), pltpu.VMEM...  16.8 us
    pallas_call x1, Pallas kernels, per_device(): pl.pallas_call(store, out_shape=(jax.ShapeDtypeStruct(fine.shape, F32), j...  0.72 us

profile of v6, /device:TPU:1, one launch (start us, length us, event | category | flops | bytes accessed | tf_op | source)
XLA Modules:
  0.0 18.2 jit_solution(16695454383372795429)
XLA Ops:
  0.6 16.8 %shard_map.77 = (f32[3,4,16,256]{3,2,1,0:T(8,128)S(1)}, f32[3,8,8,128]{3,2,1,0:T(8,128)S(1)}) custom-call(f32[3,4,16,256]{3,2,1,0:T(8,128)} %fine_now.1, f32[3,4,16,256]{3,2,1,0:T(8,128)} %fine_before.1, f32[4,4,16,256]{3,2,1,0:T(8,128)} %fine_material.1, f32[3,8,8,128]{3,2,1,0:T(8,128)} %coarse_now.1, f32[3,8,8,128]{3,2,1,0:T(8,128)} %coarse_before.1, ...), custom_call_target="tpu_custom_call" | custom-call | tf_op jit(solution)/shard_map/pallas_call | solution.py:597
  17.5 0.7 %shard_map.78 = (f32[3,4,16,256]{3,2,1,0:T(8,128)}, f32[3,8,8,128]{3,2,1,0:T(8,128)}) custom-call(f32[3,4,16,256]{3,2,1,0:T(8,128)S(1)} %get-tuple-element.4.fine, f32[3,8,8,128]{3,2,1,0:T(8,128)S(1)} %get-tuple-element.5.coarse), custom_call_target="tpu_custom_call" | custom-call | tf_op jit(solution)/shard_map/pallas_call | solution.py:587

commit v7 on v6

--- a/solution.py
+++ b/solution.py
@@ -22,7 +22,8 @@
 X_LOW_FIRST = X_COARSE + 10 * 8
 X_HIGH_FIRST = X_EXTRA + 2 * 16
 X_REST = 4 * 16 + 4 * 8
-X_LOW_ROWS = X_LOW_FIRST + X_REST
+X_LOW_REST = 2 * 16 + 4 * 8
+X_LOW_ROWS = X_LOW_FIRST + X_LOW_REST
 X_ROWS = X_HIGH_FIRST + X_REST
 Y_FINE = 32
 Y_COARSE = 24
@@ -173,7 +174,13 @@
             up = t if l == 0 else jnp.where(row8 // 2 == l, t, up)
             down = t if l == 0 else jnp.where(row8 // 2 == l - 1, t, down)
         store(high, fine_at(g, X_HIGH_FIRST), up)
-        store(low, fine_at(g, X_LOW_FIRST), down)
+        if g < 6:
+            store(low, g * 16, down)
+    for pair in range(2):
+        for k in range(8):
+            t = turned(qf[6 + 2 * pair + k // 4, k % 4 + 1, 16:24, 128:], k, 0)
+            down = t if k == 0 else jnp.where(row8 == k - 1, t, down)
+        store(low, X_LOW_FIRST + pair * 16, down)
     for q in range(5):
         for half in range(2):
             for l in range(4):
@@ -195,7 +202,7 @@
             up = t if l == 0 else jnp.where(crow == l, t, up)
             down = t if l == 0 else jnp.where(crow == l - 1, t, down)
         high[pl.ds(X_HIGH_FIRST + 64 + q * 8, 8), :] = up
-        low[pl.ds(X_LOW_FIRST + 64 + q * 8, 8), :] = down
+        low[pl.ds(X_LOW_FIRST + 32 + q * 8, 8), :] = down
     more = [jnp.where(row8 < 2, turned(qf[c, 3, 8:16, 128:], -2, 0), qf[c, 4, 8:16, 128:]) for c in range(3)]
     store(high, X_EXTRA, jnp.where(row8 < 4, more[0], turned(more[1], 4, 0)))
     store(high, X_EXTRA + 16, more[2])
@@ -210,10 +217,11 @@
 
     for g in range(6) if first else range(6, FQ):
         up = load(high, fine_at(g, X_HIGH_FIRST))
-        down = load(low, fine_at(g, X_LOW_FIRST))
+        down = load(low, g * 16 if g < 6 else X_LOW_FIRST + (g - 6) // 2 * 16)
         more = turned(load(high, X_EXTRA + g // 2 * 16), -4 * (g % 2), 0) if g < 3 else None
         for l in range(FL):
-            t = jnp.where(row8 < 4, turned(up, -2 * l, 0), turned(down, -2 * l, 0))
+            back = 2 * l if g < 6 else (g - 6) % 2 * 4 + l
+            t = jnp.where(row8 < 4, turned(up, -2 * l, 0), turned(down, -back, 0))
             if g < 3 and l == 2:
                 t = jnp.where(row8 // 2 == 1, turned(more, 2, 0), t)
             if g < 3 and l == 3:
@@ -230,7 +238,7 @@
                 qc[q, half * 4 + l + 1, 0:8, 128:] = t
     for q in () if first else range(4):
         up = high[pl.ds(X_HIGH_FIRST + 64 + q * 8, 8), :]
-        down = low[pl.ds(X_LOW_FIRST + 64 + q * 8, 8), :]
+        down = low[pl.ds(X_LOW_FIRST + 32 + q * 8, 8), :]
         for l in range(8):
             qc[5 + q, l + 1, 0:8, 128:] = jnp.where(crow < 4, turned(up, -l, 0), turned(down, -l, 0))
 
@@ -429,7 +437,7 @@
     pl.semaphore_wait(barrier, expected)
 
     high_first, high_rest = pl.ds(0, X_HIGH_FIRST), pl.ds(X_HIGH_FIRST, X_REST)
-    low_first, low_rest = pl.ds(0, X_LOW_FIRST), pl.ds(X_LOW_FIRST, X_REST)
+    low_first, low_rest = pl.ds(0, X_LOW_FIRST), pl.ds(X_LOW_FIRST, X_LOW_REST)
     messages = [
         (0, sx_high.at[high_first], rx_high.at[high_first]), (1, sx_low.at[low_first], rx_low.at[low_first]),
         (2, sy, ry.at[1]), (3, sy, ry.at[0]),

time: 18.3 us -> 18.3 us (level)
  no operation moved by 1% of the time
where the time goes in v7:
time: 18.3 us; the launch traced here: 18.2 us
  Pallas kernels  17.5 us (96%)
  between operations  0.64 us (3%)
    pallas_call x1, Pallas kernels, stepped(): pl.pallas_call(kernel, out_shape=(pltpu.VMEM(fine.shape, F32), pltpu.VMEM...  16.8 us
    pallas_call x1, Pallas kernels, per_device(): pl.pallas_call(store, out_shape=(jax.ShapeDtypeStruct(fine.shape, F32), j...  0.72 us

profile of v7, /device:TPU:1, one launch (start us, length us, event | category | flops | bytes accessed | tf_op | source)
XLA Modules:
  0.0 18.2 jit_solution(9789052862168755823)
XLA Ops:
  0.6 16.8 %shard_map.77 = (f32[3,4,16,256]{3,2,1,0:T(8,128)S(1)}, f32[3,8,8,128]{3,2,1,0:T(8,128)S(1)}) custom-call(f32[3,4,16,256]{3,2,1,0:T(8,128)} %fine_now.1, f32[3,4,16,256]{3,2,1,0:T(8,128)} %fine_before.1, f32[4,4,16,256]{3,2,1,0:T(8,128)} %fine_material.1, f32[3,8,8,128]{3,2,1,0:T(8,128)} %coarse_now.1, f32[3,8,8,128]{3,2,1,0:T(8,128)} %coarse_before.1, ...), custom_call_target="tpu_custom_call" | custom-call | tf_op jit(solution)/shard_map/pallas_call | solution.py:605
  17.4 0.7 %shard_map.78 = (f32[3,4,16,256]{3,2,1,0:T(8,128)}, f32[3,8,8,128]{3,2,1,0:T(8,128)}) custom-call(f32[3,4,16,256]{3,2,1,0:T(8,128)S(1)} %get-tuple-element.4.fine, f32[3,8,8,128]{3,2,1,0:T(8,128)S(1)} %get-tuple-element.5.coarse), custom_call_target="tpu_custom_call" | custom-call | tf_op jit(solution)/shard_map/pallas_call | solution.py:595
